TPU v7x, 32 devices: a whole 2x2x4 slice. The times are simulated.
32 devices in a mesh: seq: 8 (over z, x), head: 4 (over y, core).
Axes of the slice: x: 2, y: 2, z: 4, core: 2. Of those that a mesh axis runs over, the one named last changes fastest.
Arguments:
- queries: bfloat16 [1024, 2560], P('seq', 'head'), may hold values from -6 to 6
- keys: bfloat16 [1024, 2560], P('seq', 'head'), may hold values from -6 to 6
- values: bfloat16 [1024, 2560], P('seq', 'head'), may hold values from -6 to 6
- head_class: int32 [20], replicated, may hold values from 0 to 1, as said below
- window_lengths: int32 [8, 4], P('seq'), may hold values from 1 to 64, 128 in all within a row
- out_weight: bfloat16 [2560, 5120], P('seq', 'head'), may hold values from -0.125 to 0.125
Outputs:
- projected: bfloat16 [1024, 5120], P('seq', 'head')
Inputs may be any that keep to these rules, and one draw needn't show every extreme that they name: `head_class`: each group of 5 consecutive heads holds 1 to 3 temporal heads, and some group holds exactly 3. `window_lengths`: the 4 lengths of each block sum to 128, and the longest is exactly 64.
All inputs are finite; a program needn't handle non-finite values.
Results may differ from a plain program's by a relative error of at most 0.0057.
Values may be sent and summed in bfloat16 or wider, within the bound.
A program may use at most 64 MiB of HBM per device.

v0:
```python
import math

import jax
import jax.numpy as jnp
from jax import lax
from jax.sharding import PartitionSpec as P

HD = 128
TMAX = 3
FRAMES = 8


def softmax_rows(scores):
    highest = jnp.max(scores, axis=-1, keepdims=True)
    weights = jnp.exp(scores - highest)
    return weights / jnp.sum(weights, axis=-1, keepdims=True)


def compact_heads(source, picker):
    return jnp.einsum("shd,th->std", source, picker, preferred_element_type=jnp.float32).astype(
        jnp.bfloat16
    )


def expand_heads(source, picker):
    return jnp.einsum("std,th->shd", source, picker, preferred_element_type=jnp.float32).astype(
        jnp.bfloat16
    )


def window_attention(query, key_rows, value_rows, lengths, scaling):
    ends = jnp.cumsum(lengths)
    positions = jnp.arange(query.shape[0], dtype=jnp.int32)
    window_ids = jnp.sum((positions[:, None] >= ends[None, :]).astype(jnp.int32), axis=1)
    same_window = window_ids[:, None] == window_ids[None, :]
    scores = (
        jnp.einsum("shd,thd->hst", query, key_rows, preferred_element_type=jnp.float32) * scaling
    )
    scores = jnp.where(same_window[None], scores, -1e30)
    weights = softmax_rows(scores).astype(jnp.bfloat16)
    return jnp.einsum(
        "hst,thd->shd", weights, value_rows, preferred_element_type=jnp.float32
    ).astype(jnp.bfloat16)


def body(queries, keys, values, head_class, window_lengths, out_weight):
    tok_len, columns = queries.shape
    local_heads = columns // HD
    scaling = 1.0 / math.sqrt(HD)
    head_group = lax.axis_index("head")
    classes = lax.dynamic_slice_in_dim(head_class, head_group * local_heads, local_heads)
    temporal_mask = classes == 1
    slot_rank = jnp.cumsum(temporal_mask.astype(jnp.int32)) - 1
    slot_ids = jnp.arange(TMAX, dtype=jnp.int32)
    picker = ((slot_rank[None, :] == slot_ids[:, None]) & temporal_mask[None, :]).astype(
        jnp.bfloat16
    )
    shaped = [array_in.reshape(tok_len, local_heads, HD) for array_in in (queries, keys, values)]
    lengths = window_lengths[0]
    spatial_out = window_attention(shaped[0], shaped[1], shaped[2], lengths, scaling)
    packed = [compact_heads(array_in, picker)[None] for array_in in shaped]
    query = lax.all_to_all(packed[0], "seq", split_axis=1, concat_axis=0, tiled=True)
    key_rows = lax.all_to_all(packed[1], "seq", split_axis=1, concat_axis=0, tiled=True)
    value_rows = lax.all_to_all(packed[2], "seq", split_axis=1, concat_axis=0, tiled=True)
    sources, width, count, size = query.shape
    groups = sources // FRAMES
    query = query.reshape(FRAMES, groups, width, count, size)
    key_rows = key_rows.reshape(FRAMES, groups, width, count, size)
    value_rows = value_rows.reshape(FRAMES, groups, width, count, size)
    scores = (
        jnp.einsum("fjcnd,gjcnd->jcnfg", query, key_rows, preferred_element_type=jnp.float32)
        * scaling
    )
    weights = softmax_rows(scores).astype(jnp.bfloat16)
    attended = jnp.einsum(
        "jcnfg,gjcnd->fjcnd", weights, value_rows, preferred_element_type=jnp.float32
    ).astype(jnp.bfloat16)
    attended = attended.reshape(sources, width, count, size)
    returned = lax.all_to_all(attended, "seq", split_axis=0, concat_axis=1, tiled=True)
    temporal_out = expand_heads(returned[0], picker)
    mixed = jnp.where(temporal_mask[None, :, None], temporal_out, spatial_out)
    mixed_local = mixed.reshape(tok_len, local_heads * HD)
    mixed_all = lax.all_gather(mixed_local, "head", axis=1, tiled=True)
    summed = jnp.dot(
        mixed_all,
        lax.all_gather(out_weight, "seq", axis=0, tiled=True),
        preferred_element_type=jnp.float32,
    )
    return summed.astype(jnp.bfloat16)


def solution(mesh):
    placed = (
        P("seq", "head"),
        P("seq", "head"),
        P("seq", "head"),
        P(),
        P("seq", None),
        P("seq", "head"),
    )
    return jax.shard_map(
        body, mesh=mesh, in_specs=placed, out_specs=P("seq", "head"), check_vma=False
    )
```

profile of v0, /device:TPU:0, one launch (start us, length us, event | category | flops | bytes accessed | tf_op | source)
XLA Modules:
  0.0 131.6 jit_solution(468909702398699324)
XLA Ops:
  6.5 0.7 all-gather.2.cloned.1.call-update
  7.3 0.7 convert_bitcast_fusion
  8.2 1.1 copy.103
  9.5 0.9 fusion.10
  10.3 7.3 %all-to-all-start.1 = ((bf16[1,128,3,128]{3,2,0,1:T(4,128)(2,1)}), bf16[1,128,3,128]{3,2,0,1:T(4,128)(2,1)S(1)}, u32[]{:S(2)}, u32[]{:S(2)}) async-start(bf16[1,128,3,128]{3,2,0,1:T(4,128)(2,1)} %fusion.10), calls=%async_computation.1 | async-start | bytes 262144 | tf_op jit(solution)/shard_map/all_to_all | solution.py:62
  17.6 1.1 copy.107
  18.7 0.8 reduce-window.17
  20.1 1.1 copy.99
  21.5 0.9 fusion.11
  22.3 2.7 %all-to-all-done.1 = bf16[1,128,3,128]{3,2,0,1:T(4,128)(2,1)S(1)} async-done(((bf16[1,128,3,128]{3,2,0,1:T(4,128)(2,1)}), bf16[1,128,3,128]{3,2,0,1:T(4,128)(2,1)S(1)}, u32[]{:S(2)}, u32[]{:S(2)}) %all-to-all-start.1) | async-done | bytes 98336 | tf_op jit(solution)/shard_map/all_to_all | solution.py:62
  25.0 3.4 %all-to-all-start.2 = ((bf16[1,128,3,128]{3,2,0,1:T(4,128)(2,1)}), bf16[1,128,3,128]{3,2,0,1:T(4,128)(2,1)S(1)}, u32[]{:S(2)}, u32[]{:S(2)}) async-start(bf16[1,128,3,128]{3,2,0,1:T(4,128)(2,1)} %fusion.11), calls=%async_computation.2 | async-start | bytes 262144 | tf_op jit(solution)/shard_map/all_to_all | solution.py:63
  28.4 0.9 fusion.9
  29.4 9.0 %all-to-all-done.2 = bf16[1,128,3,128]{3,2,0,1:T(4,128)(2,1)S(1)} async-done(((bf16[1,128,3,128]{3,2,0,1:T(4,128)(2,1)}), bf16[1,128,3,128]{3,2,0,1:T(4,128)(2,1)S(1)}, u32[]{:S(2)}, u32[]{:S(2)}) %all-to-all-start.2) | async-done | bytes 98336 | tf_op jit(solution)/shard_map/all_to_all | solution.py:63
  38.4 3.4 %all-to-all-start = ((bf16[1,128,3,128]{3,2,0,1:T(4,128)(2,1)}), bf16[1,128,3,128]{3,2,0,1:T(4,128)(2,1)S(1)}, u32[]{:S(2)}, u32[]{:S(2)}) async-start(bf16[1,128,3,128]{3,2,0,1:T(4,128)(2,1)} %fusion.9), calls=%async_computation | async-start | bytes 262144 | tf_op jit(solution)/shard_map/all_to_all | solution.py:64
  42.0 0.3 fusion.33
  42.3 9.1 %all-to-all-done = bf16[1,128,3,128]{3,2,0,1:T(4,128)(2,1)S(1)} async-done(((bf16[1,128,3,128]{3,2,0,1:T(4,128)(2,1)}), bf16[1,128,3,128]{3,2,0,1:T(4,128)(2,1)S(1)}, u32[]{:S(2)}, u32[]{:S(2)}) %all-to-all-start) | async-done | bytes 98336 | tf_op jit(solution)/shard_map/all_to_all | solution.py:64
  51.4 0.3 fusion.12
  51.7 0.7 copy.115
  52.3 4.3 %all-to-all-start.3 = ((bf16[8,16,3,128]{3,1,2,0:T(8,128)(2,1)}), bf16[8,16,3,128]{3,1,2,0:T(8,128)(2,1)S(1)}, u32[]{:S(2)}, u32[]{:S(2)}) async-start(bf16[8,16,3,128]{3,1,2,0:T(8,128)(2,1)} %copy.115), calls=%async_computation.3 | async-start | bytes 196608 | tf_op jit(solution)/shard_map/all_to_all | solution.py:79
  57.1 6.8 %all-to-all-done.3 = bf16[8,16,3,128]{3,1,2,0:T(8,128)(2,1)S(1)} async-done(((bf16[8,16,3,128]{3,1,2,0:T(8,128)(2,1)}), bf16[8,16,3,128]{3,1,2,0:T(8,128)(2,1)S(1)}, u32[]{:S(2)}, u32[]{:S(2)}) %all-to-all-start.3) | async-done | bytes 98336 | tf_op jit(solution)/shard_map/all_to_all | solution.py:79
  63.9 0.3 fusion.7
  64.4 7.9 %all_gather.6 = bf16[128,2560]{0,1:T(8,128)(2,1)S(1)} all-gather(bf16[128,640]{0,1:T(8,128)(2,1)S(1)} %bitcast.63), channel_id=1, replica_groups=mesh['seq'=8,'head'=4] {'head'}, dimensions={1}, use_global_device_ids=true | all-gather | bytes 819200 | tf_op jit(solution)/shard_map/all_gather | solution.py:83
  72.2 47.8 %all-gather.2.cloned.1.call-done = bf16[2560,1280]{1,0:T(8,128)(2,1)} async-done(((bf16[320,1280]{1,0:T(8,128)(2,1)}), bf16[2560,1280]{1,0:T(8,128)(2,1)}) %all-gather.2.cloned.1.call-update) | async-done | bytes 6553616 | tf_op jit(solution)/shard_map/all_gather | solution.py:86
  120.1 4.6 %convolution_convert_fusion = bf16[128,1280]{1,0:T(8,128)(2,1)} fusion(bf16[128,2560]{0,1:T(8,128)(2,1)S(1)} %all_gather.6, bf16[2560,1280]{1,0:T(8,128)(2,1)} %all-gather.2.cloned.1.call-done), kind=kOutput, calls=%fused_computation.2 | convolution fusion | flops 839024640 | bytes 7536640 | tf_op jit(solution)/shard_map/dot_general | solution.py:84
  (15 shorter events, 2.2 us)
Async XLA Ops:
  6.5 113.5 %all-gather.2.cloned.1.call-start = ((), (), s32[]{:S(2)}) async-start(), calls=%async_computation.4 | async-start | bytes 7372800 | tf_op jit(solution)/shard_map/all_gather | solution.py:86
  10.3 14.7 %all-to-all-start.1 = ((bf16[1,128,3,128]{3,2,0,1:T(4,128)(2,1)}), bf16[1,128,3,128]{3,2,0,1:T(4,128)(2,1)S(1)}, u32[]{:S(2)}, u32[]{:S(2)}) async-start(bf16[1,128,3,128]{3,2,0,1:T(4,128)(2,1)} %fusion.10), calls=%async_computation.1 | async-start | bytes 262144 | tf_op jit(solution)/shard_map/all_to_all | solution.py:62
  25.0 13.3 %all-to-all-start.2 = ((bf16[1,128,3,128]{3,2,0,1:T(4,128)(2,1)}), bf16[1,128,3,128]{3,2,0,1:T(4,128)(2,1)S(1)}, u32[]{:S(2)}, u32[]{:S(2)}) async-start(bf16[1,128,3,128]{3,2,0,1:T(4,128)(2,1)} %fusion.11), calls=%async_computation.2 | async-start | bytes 262144 | tf_op jit(solution)/shard_map/all_to_all | solution.py:63
  38.4 13.0 %all-to-all-start = ((bf16[1,128,3,128]{3,2,0,1:T(4,128)(2,1)}), bf16[1,128,3,128]{3,2,0,1:T(4,128)(2,1)S(1)}, u32[]{:S(2)}, u32[]{:S(2)}) async-start(bf16[1,128,3,128]{3,2,0,1:T(4,128)(2,1)} %fusion.9), calls=%async_computation | async-start | bytes 262144 | tf_op jit(solution)/shard_map/all_to_all | solution.py:64
  52.3 11.5 %all-to-all-start.3 = ((bf16[8,16,3,128]{3,1,2,0:T(8,128)(2,1)}), bf16[8,16,3,128]{3,1,2,0:T(8,128)(2,1)S(1)}, u32[]{:S(2)}, u32[]{:S(2)}) async-start(bf16[8,16,3,128]{3,1,2,0:T(8,128)(2,1)} %copy.115), calls=%async_computation.3 | async-start | bytes 196608 | tf_op jit(solution)/shard_map/all_to_all | solution.py:79
Sparse Core Ops, SparseCore 0:
  9.5 110.4 all-gather.1
where the time goes:
time: 132 us
  waiting for transfers between devices  76.1 us (58%)
  starting transfers between devices  18.3 us (14%)
  between operations  13.5 us (10%)
  matrix products  8.89 us (7%)
  blocking collectives  7.89 us (6%)
  local copies, waits for them, and re-layouts  4.93 us (4%)
  other arithmetic  2.02 us (2%)
    all_gather x1, waiting for transfers between devices, body(): lax.all_gather(out_weight, 'seq', axis=0, tiled=True)  47.8 us
    all_to_all x1, waiting for transfers between devices, body(): lax.all_to_all(packed[2], 'seq', split_axis=1, concat_axis=0, tiled=True)  9.05 us
    all_to_all x1, waiting for transfers between devices, body(): lax.all_to_all(packed[1], 'seq', split_axis=1, concat_axis=0, tiled=True)  8.99 us
    all_gather x1, blocking collectives, body(): mixed_all = lax.all_gather(mixed_local, 'head', axis=1, tiled=True)  7.89 us
    all_to_all x1, starting transfers between devices, body(): lax.all_to_all(packed[0], 'seq', split_axis=1, concat_axis=0, tiled=True)  7.25 us
    all_to_all x1, waiting for transfers between devices, body(): lax.all_to_all(attended, 'seq', split_axis=0, concat_axis=1, tiled=True)  6.79 us
    dot_general x1, matrix products, body(): jnp.dot(mixed_all, lax.all_gather(out_weight, 'seq', axis=0, tiled=True),...  4.65 us
    all_to_all x1, starting transfers between devices, body(): lax.all_to_all(attended, 'seq', split_axis=0, concat_axis=1, tiled=True)  4.29 us
  transfers between devices with their start and end apart: 5, of which 5 were waited for; matrix products, arithmetic and copies ran while one was open for 9% of the time, Pallas kernels for 0%

commit v1 on v0

--- a/solution.py
+++ b/solution.py
@@ -1,8 +1,11 @@
+import functools
 import math
 
 import jax
 import jax.numpy as jnp
 from jax import lax
+from jax.experimental import pallas as pl
+from jax.experimental.pallas import tpu as pltpu
 from jax.sharding import PartitionSpec as P
 
 HD = 128
@@ -43,7 +46,7 @@
     ).astype(jnp.bfloat16)
 
 
-def body(queries, keys, values, head_class, window_lengths, out_weight):
+def gather_body(queries, keys, values, head_class, window_lengths, out_weight):
     tok_len, columns = queries.shape
     local_heads = columns // HD
     scaling = 1.0 / math.sqrt(HD)
@@ -89,7 +92,324 @@
     return summed.astype(jnp.bfloat16)
 
 
+MESH = pl.DeviceIdType.MESH
+CHUNKS = 2
+
+
+def masked_attention(query, key_rows, value_rows, same, scaling):
+    scores = lax.dot_general(
+        query, key_rows, (((1,), (1,)), ((), ())), preferred_element_type=jnp.float32
+    )
+    scores = jnp.where(same, scores * scaling, -1e30)
+    weights = softmax_rows(scores).astype(jnp.bfloat16)
+    return jnp.dot(weights, value_rows, preferred_element_type=jnp.float32).astype(jnp.bfloat16)
+
+
+def slot_conditions(class_ref, first, local_heads):
+    rank = jnp.int32(0)
+    taken = []
+    for h in range(local_heads):
+        flag = (class_ref[first + h] == 1).astype(jnp.int32)
+        taken.append([flag * (rank == t).astype(jnp.int32) == 1 for t in range(TMAX)])
+        rank = rank + flag
+    return taken
+
+
+def layer_kernel(
+    n, groups, class_ref, len_ref, q_ref, k_ref, v_ref, w_ref, out_ref,
+    packed, landed, spat, spat_in, tsend, temp_in, mixed, w_all,
+    up_in, up_out, down_in, down_out,
+    qkv_s, qkv_r, w_s, w_r, w_l, sp_s, sp_r, sp_l, spf_s, t_s, t_r, t_l, tf_s,
+    up_s, up_r, down_s, down_r,
+):
+    pair = n // groups
+    seq, head = lax.axis_index("seq"), lax.axis_index("head")
+    plane, lane = seq // pair, lax.rem(seq, pair)
+    core = lax.rem(head, 2)
+    sibling = head + 1 - 2 * core
+    tok, columns = q_ref.shape
+    local_heads = columns // HD
+    width = tok // n
+    rows = w_ref.shape[0]
+    scaling = 1.0 / math.sqrt(HD)
+
+    def send(src, dst, send_sem, recv_sem, to_seq, to_head):
+        return pltpu.make_async_remote_copy(
+            src_ref=src, dst_ref=dst, send_sem=send_sem, recv_sem=recv_sem,
+            device_id=(to_seq, to_head), device_id_type=MESH,
+        )
+
+    own_w = pltpu.make_async_copy(w_ref, w_all.at[lane], w_l)
+    own_w.start()
+
+    barrier = pltpu.get_barrier_semaphore()
+
+    def greet(to_seq, to_head):
+        pl.semaphore_signal(barrier, inc=1, device_id=(to_seq, to_head), device_id_type=MESH)
+
+    for step in range(1, n):
+        greet(lax.rem(seq + step, n), head)
+    greet(seq, sibling)
+
+    @pl.when(plane != head)
+    def _():
+        for peer in range(n):
+            greet(jnp.int32(peer), plane)
+
+    taken = slot_conditions(class_ref, head * local_heads, local_heads)
+    for a, ref in enumerate((q_ref, k_ref, v_ref)):
+        for t in range(TMAX):
+            value = jnp.zeros((tok, HD), jnp.bfloat16)
+            for h in range(t, local_heads):
+                value = jnp.where(taken[h][t], ref[:, h * HD:(h + 1) * HD], value)
+            at = (a * TMAX + t) * HD
+            packed[:, :, at:at + HD] = value.reshape(n, width, HD)
+
+    @pl.when(plane == 0)
+    def _():
+        up_in[...] = jnp.zeros_like(up_in)
+
+    @pl.when(plane == groups - 1)
+    def _():
+        down_in[...] = jnp.zeros_like(down_in)
+
+    pl.semaphore_wait(barrier, (n - 1) + pair * (groups - 1) + 1)
+
+    qkv = []
+    for step in range(1, n):
+        peer = lax.rem(seq + step, n)
+        copy = send(packed.at[peer], landed.at[seq], qkv_s.at[peer], qkv_r.at[seq], peer, head)
+        copy.start()
+        qkv.append(copy)
+    landed[seq] = packed[seq]
+
+    other = plane * pair + (1 - lane)
+    w_copy = send(w_ref, w_all.at[lane], w_s, w_r.at[lane], other, head)
+    w_copy.start()
+
+    def window_of(axis):
+        position = lax.broadcasted_iota(jnp.int32, (tok, tok), axis)
+        ids = jnp.zeros((tok, tok), jnp.int32)
+        end = jnp.int32(0)
+        for i in range(len_ref.shape[1]):
+            end = end + len_ref[0, i]
+            ids = ids + (position >= end).astype(jnp.int32)
+        return ids
+
+    same_window = window_of(0) == window_of(1)
+    for h in range(local_heads):
+        at = slice(h * HD, (h + 1) * HD)
+        spat[:, at] = masked_attention(q_ref[:, at], k_ref[:, at], v_ref[:, at], same_window, scaling)
+
+    sp_core = lax.rem(plane, 2)
+    sp_copies = []
+    for y in range(groups // 2):
+        to_seq, to_head = head * pair + lane, 2 * y + sp_core
+        mine = (to_seq == seq) & (to_head == head)
+        copy = send(spat, spat_in.at[plane], sp_s.at[y], sp_r.at[plane], to_seq, to_head)
+        sp_copies.append((mine, copy))
+
+        @pl.when(jnp.logical_not(mine))
+        def _(copy=copy):
+            copy.start()
+
+        @pl.when(mine)
+        def _():
+            spat_in[plane] = spat[...]
+
+    for step in range(1, n):
+        peer = lax.rem(seq + n - step, n)
+        send(landed.at[peer], landed.at[peer], qkv_s.at[peer], qkv_r.at[peer], peer, head).wait_recv()
+    row = lax.rem(lax.broadcasted_iota(jnp.int32, (tok, tok), 0), width)
+    column = lax.rem(lax.broadcasted_iota(jnp.int32, (tok, tok), 1), width)
+    same_position = row == column
+    for t in range(TMAX):
+        query, key_rows, value_rows = (
+            landed[:, :, (a * TMAX + t) * HD:(a * TMAX + t + 1) * HD].reshape(tok, HD)
+            for a in range(3)
+        )
+        result = masked_attention(query, key_rows, value_rows, same_position, scaling)
+        for f in range(n):
+            tsend[f % pair, f // pair, :, t * HD:(t + 1) * HD] = result[f * width:(f + 1) * width]
+
+    t_core = lax.rem(seq, 2)
+    t_copies = []
+    for x in range(pair):
+        for y in range(groups // 2):
+            to_seq, to_head = head * pair + x, 2 * y + t_core
+            mine = (to_seq == seq) & (to_head == head)
+            copy = send(tsend.at[x], temp_in.at[seq], t_s.at[x, y], t_r.at[seq], to_seq, to_head)
+            t_copies.append((mine, copy))
+
+            @pl.when(jnp.logical_not(mine))
+            def _(copy=copy):
+                copy.start()
+
+            @pl.when(mine)
+            def _(x=x):
+                temp_in[seq] = tsend[x]
+
+    forwards = []
+    for j in range(groups // 2):
+        source = 2 * j + core
+        here = (source == plane) & (plane == head)
+        copy = send(spat_in.at[source], spat_in.at[source], spf_s.at[j], sp_r.at[source], seq, sibling)
+
+        @pl.when(jnp.logical_not(here))
+        def _(copy=copy):
+            copy.wait_recv()
+
+        copy.start()
+        forwards.append(copy)
+    for j in range(n // 2):
+        source = 2 * j + core
+        here = (source == seq) & (plane == head)
+        copy = send(temp_in.at[source], temp_in.at[source], tf_s.at[j], t_r.at[source], seq, sibling)
+
+        @pl.when(jnp.logical_not(here))
+        def _(copy=copy):
+            copy.wait_recv()
+
+        copy.start()
+        forwards.append(copy)
+    for j in range(groups // 2):
+        source = 2 * j + 1 - core
+        send(spat_in.at[source], spat_in.at[source], spf_s.at[j], sp_r.at[source], seq, sibling).wait_recv()
+    for j in range(n // 2):
+        source = 2 * j + 1 - core
+        send(temp_in.at[source], temp_in.at[source], tf_s.at[j], t_r.at[source], seq, sibling).wait_recv()
+
+    taken = slot_conditions(class_ref, plane * local_heads, local_heads)
+    for z in range(groups):
+        for h in range(local_heads):
+            value = spat_in[z, :, h * HD:(h + 1) * HD]
+            for t in range(min(h + 1, TMAX)):
+                slot = temp_in[:, z, :, t * HD:(t + 1) * HD].reshape(tok, HD)
+                value = jnp.where(taken[h][t], slot, value)
+            mixed[z, :, h * HD:(h + 1) * HD] = value
+
+    own_w.wait()
+    send(w_ref, w_all.at[1 - lane], w_s, w_r.at[1 - lane], other, head).wait_recv()
+
+    chunk = w_ref.shape[1] // CHUNKS
+
+    def product(z, c):
+        weight = w_all[:, :, c * chunk:(c + 1) * chunk].reshape(pair * rows, chunk)
+        return jnp.dot(mixed[z], weight, preferred_element_type=jnp.float32)
+
+    ways = ((1, up_in, up_out, up_s, up_r), (-1, down_in, down_out, down_s, down_r))
+
+    def onward(way, d, c):
+        sign, came, goes, s_sem, r_sem = way
+        to_seq = seq + sign * pair
+        return send(goes.at[d - 1, c], came.at[d - 1, c], s_sem.at[d - 1, c], r_sem.at[d - 1, c], to_seq, head)
+
+    def has_previous(way):
+        return plane > 0 if way[0] == 1 else plane < groups - 1
+
+    def reaches(way, d):
+        return plane + d < groups if way[0] == 1 else plane >= d
+
+    def arrive(way, d, c):
+        @pl.when(has_previous(way))
+        def _():
+            sign, came, goes, s_sem, r_sem = way
+            send(goes.at[d, c], came.at[d, c], s_sem.at[d, c], r_sem.at[d, c], seq, head).wait_recv()
+
+    for d in range(groups - 1, 0, -1):
+        for c in range(CHUNKS):
+            for way in ways:
+                @pl.when(reaches(way, d))
+                def _(way=way, d=d, c=c):
+                    total = product(plane + way[0] * d, c)
+                    if d < groups - 1:
+                        arrive(way, d, c)
+                        total = total + way[1][d, c].astype(jnp.float32)
+                    way[2][d - 1, c] = total.astype(jnp.bfloat16)
+                    onward(way, d, c).start()
+    for c in range(CHUNKS):
+        total = product(plane, c)
+        for way in ways:
+            arrive(way, 0, c)
+            total = total + way[1][0, c].astype(jnp.float32)
+        out_ref[:, c * chunk:(c + 1) * chunk] = total.astype(jnp.bfloat16)
+
+    for copy in qkv:
+        copy.wait_send()
+    w_copy.wait_send()
+    for mine, copy in sp_copies + t_copies:
+        @pl.when(jnp.logical_not(mine))
+        def _(copy=copy):
+            copy.wait_send()
+    for copy in forwards:
+        copy.wait_send()
+    for d in range(groups - 1, 0, -1):
+        for c in range(CHUNKS):
+            for way in ways:
+                @pl.when(reaches(way, d))
+                def _(way=way, d=d, c=c):
+                    onward(way, d, c).wait_send()
+
+
+def kernel_body(n, groups, queries, keys, values, head_class, window_lengths, out_weight):
+    tok, columns = queries.shape
+    rows, out_columns = out_weight.shape
+    pair, width = n // groups, tok // n
+    chunk = out_columns // CHUNKS
+    bf16, dma = jnp.bfloat16, pltpu.SemaphoreType.DMA
+    vmem = pl.BlockSpec(memory_space=pltpu.VMEM)
+    smem = pl.BlockSpec(memory_space=pltpu.SMEM)
+    line = (groups - 1, CHUNKS)
+    return pl.pallas_call(
+        functools.partial(layer_kernel, n, groups),
+        out_shape=jax.ShapeDtypeStruct((tok, out_columns), bf16),
+        in_specs=[smem, smem, vmem, vmem, vmem, pl.BlockSpec(memory_space=pl.ANY)],
+        out_specs=vmem,
+        scratch_shapes=[
+            pltpu.VMEM((n, width, 3 * TMAX * HD), bf16),
+            pltpu.VMEM((n, width, 3 * TMAX * HD), bf16),
+            pltpu.VMEM((tok, columns), bf16),
+            pltpu.VMEM((groups, tok, columns), bf16),
+            pltpu.VMEM((pair, groups, width, TMAX * HD), bf16),
+            pltpu.VMEM((n, groups, width, TMAX * HD), bf16),
+            pltpu.VMEM((groups, tok, columns), bf16),
+            pltpu.VMEM((pair, rows, out_columns), bf16),
+            pltpu.VMEM(line + (tok, chunk), bf16),
+            pltpu.VMEM(line + (tok, chunk), bf16),
+            pltpu.VMEM(line + (tok, chunk), bf16),
+            pltpu.VMEM(line + (tok, chunk), bf16),
+            dma((n,)), dma((n,)),
+            dma, dma((pair,)), dma,
+            dma((groups // 2,)), dma((groups,)), dma, dma((groups // 2,)),
+            dma((pair, groups // 2)), dma((n,)), dma, dma((n // 2,)),
+            dma(line), dma(line), dma(line), dma(line),
+        ],
+        compiler_params=pltpu.CompilerParams(
+            collective_id=0, has_side_effects=True, vmem_limit_bytes=32 * 1024 * 1024
+        ),
+        cost_estimate=pl.CostEstimate(
+            flops=2 * groups * tok * columns * out_columns,
+            bytes_accessed=4 * rows * out_columns,
+            transcendentals=local_count(columns) * tok * tok,
+        ),
+    )(head_class, window_lengths, queries, keys, values, out_weight)
+
+
+def local_count(columns):
+    return columns // HD + TMAX
+
+
 def solution(mesh):
+    n, groups = mesh.shape["seq"], mesh.shape["head"]
+
+    def body(queries, keys, values, head_class, window_lengths, out_weight):
+        tok, rows = queries.shape[0], out_weight.shape[0]
+        if n == FRAMES and n == 2 * groups and rows > tok:
+            return kernel_body(
+                n, groups, queries, keys, values, head_class, window_lengths, out_weight
+            )
+        return gather_body(queries, keys, values, head_class, window_lengths, out_weight)
+
     placed = (
         P("seq", "head"),
         P("seq", "head"),

time: 132 us -> 66.1 us (0.50)
  waiting for transfers between devices: 76.1 us -> 0 us
  Pallas kernels: 0 us -> 59 us
  starting transfers between devices: 18.3 us -> 0 us
  between operations: 13.5 us -> 0.02 us
  matrix products: 8.89 us -> 0 us
  blocking collectives: 7.89 us -> 0 us
  other arithmetic: 2.02 us -> 0 us
    pallas_call x0 -> x1, Pallas kernels: none -> 59 us  [kernel_body(): pl.pallas_call(functools.partial(layer_kernel, n, groups), out_shape=jax....]
    all_gather x1 -> x0, waiting for transfers between devices: 47.8 us -> none  [body(): lax.all_gather(out_weight, 'seq', axis=0, tiled=True)]
    all_to_all x4 -> x0, waiting for transfers between devices: 27.6 us -> none  [the longest x1 9.05 us: body(): lax.all_to_all(packed[2], 'seq', split_axis=1, concat_axis=0, tiled=True)]
    all_to_all x4 -> x0, starting transfers between devices: 18.3 us -> none  [the longest x1 7.25 us: body(): lax.all_to_all(packed[0], 'seq', split_axis=1, concat_axis=0, tiled=True)]
    dot_general x9 -> x0, matrix products: 8.58 us -> none  [the longest x1 4.65 us: body(): jnp.dot(mixed_all, lax.all_gather(out_weight, 'seq', axis=0, tiled=True),...]
    all_gather x1 -> x0, blocking collectives: 7.89 us -> none  [body(): mixed_all = lax.all_gather(mixed_local, 'head', axis=1, tiled=True)]
    unnamed x3 -> x13, local copies, waits for them, and re-layouts: 3.24 us -> 5.93 us
    another operation x3 -> x0, other arithmetic: 1.75 us -> none
  transfers between devices with their start and end apart: 5 -> 0, of which waited for: 5 -> 0; matrix products, arithmetic and copies ran while one was open for 9% -> 0% of each run, Pallas kernels for 0% -> 0%
where the time goes in v1:
time: 66.1 us; the launch traced here: 64.9 us
  Pallas kernels  59 us (89%)
  local copies, waits for them, and re-layouts  5.93 us (9%)
    pallas_call x1, Pallas kernels, kernel_body(): pl.pallas_call(functools.partial(layer_kernel, n, groups), out_shape=jax....  59 us
    unnamed x13, local copies, waits for them, and re-layouts  5.93 us

profile of v1, /device:TPU:0, one launch (start us, length us, event | category | flops | bytes accessed | tf_op | source)
XLA Modules:
  0.0 64.9 jit_solution(13554878958899264321)
XLA Ops:
  0.0 0.0 copy-start
  0.0 1.1 %copy-done = bf16[320,1280]{1,0:T(8,128)(2,1)S(1)} copy-done((bf16[320,1280]{1,0:T(8,128)(2,1)S(1)}, bf16[320,1280]{1,0:T(8,128)(2,1)}, u32[]{:S(2)}) %copy-start) | copy-done | bytes 819224
  1.1 0.0 copy-start.1
  1.1 0.9 %copy-done.1 = bf16[128,640]{1,0:T(8,128)(2,1)S(1)} copy-done((bf16[128,640]{1,0:T(8,128)(2,1)S(1)}, bf16[128,640]{1,0:T(8,128)(2,1)}, u32[]{:S(2)}) %copy-start.1) | copy-done | bytes 163864
  2.1 0.0 copy-start.2
  2.1 0.9 %copy-done.2 = bf16[128,640]{1,0:T(8,128)(2,1)S(1)} copy-done((bf16[128,640]{1,0:T(8,128)(2,1)S(1)}, bf16[128,640]{1,0:T(8,128)(2,1)}, u32[]{:S(2)}) %copy-start.2) | copy-done | bytes 163864
  3.0 0.0 copy-start.3
  3.0 0.9 %copy-done.3 = bf16[128,640]{1,0:T(8,128)(2,1)S(1)} copy-done((bf16[128,640]{1,0:T(8,128)(2,1)S(1)}, bf16[128,640]{1,0:T(8,128)(2,1)}, u32[]{:S(2)}) %copy-start.3) | copy-done | bytes 163864
  3.9 0.0 copy-start.4
  3.9 0.7 %copy-done.4 = s32[20]{0:T(128)S(1)} copy-done((s32[20]{0:T(128)S(1)}, s32[20]{0:T(128)}, u32[]{:S(2)}) %copy-start.4) | copy-done | bytes 104
  4.6 0.0 copy-start.5
  4.6 0.7 %copy-done.5 = s32[1,4]{1,0:T(1,128)S(1)} copy-done((s32[1,4]{1,0:T(1,128)S(1)}, s32[1,4]{1,0:T(1,128)}, u32[]{:S(2)}) %copy-start.5) | copy-done | bytes 40
  5.2 59.0 %shard_map.64 = bf16[128,1280]{1,0:T(8,128)(2,1)S(1)} custom-call(s32[20]{0:T(128)S(1)} %copy-done.4, s32[1,4]{1,0:T(1,128)S(1)} %copy-done.5, bf16[128,640]{1,0:T(8,128)(2,1)S(1)} %copy-done.1, bf16[128,640]{1,0:T(8,128)(2,1)S(1)} %copy-done.2, bf16[128,640]{1,0:T(8,128)(2,1)S(1)} %copy-done.3, bf16[320,1280]{1,0:T(8,128)(2,1)S(1)} %copy-done), custom_call_target="tpu_custom_call" | custom-call | flops 838860800 | bytes 1638400 | tf_op jit(solution)/shard_map/pallas_call | solution.py:363
  64.2 0.7 %copy.8 = bf16[128,1280]{1,0:T(8,128)(2,1)} copy(bf16[128,1280]{1,0:T(8,128)(2,1)S(1)} %shard_map.64) | data formatting | bytes 655360
Async XLA Ops:
  0.0 1.1 %copy-start = (bf16[320,1280]{1,0:T(8,128)(2,1)S(1)}, bf16[320,1280]{1,0:T(8,128)(2,1)}, u32[]{:S(2)}) copy-start(bf16[320,1280]{1,0:T(8,128)(2,1)} %w_ref.1) | copy-start | bytes 2457604
  1.1 0.9 %copy-start.1 = (bf16[128,640]{1,0:T(8,128)(2,1)S(1)}, bf16[128,640]{1,0:T(8,128)(2,1)}, u32[]{:S(2)}) copy-start(bf16[128,640]{1,0:T(8,128)(2,1)} %q_ref.1) | copy-start | bytes 491524
  2.1 0.9 %copy-start.2 = (bf16[128,640]{1,0:T(8,128)(2,1)S(1)}, bf16[128,640]{1,0:T(8,128)(2,1)}, u32[]{:S(2)}) copy-start(bf16[128,640]{1,0:T(8,128)(2,1)} %k_ref.1) | copy-start | bytes 491524
  3.0 0.9 %copy-start.3 = (bf16[128,640]{1,0:T(8,128)(2,1)S(1)}, bf16[128,640]{1,0:T(8,128)(2,1)}, u32[]{:S(2)}) copy-start(bf16[128,640]{1,0:T(8,128)(2,1)} %v_ref.1) | copy-start | bytes 491524
  3.9 0.7 %copy-start.4 = (s32[20]{0:T(128)S(1)}, s32[20]{0:T(128)}, u32[]{:S(2)}) copy-start(s32[20]{0:T(128)} %class_ref.1) | copy-start | bytes 244
  4.6 0.7 %copy-start.5 = (s32[1,4]{1,0:T(1,128)S(1)}, s32[1,4]{1,0:T(1,128)}, u32[]{:S(2)}) copy-start(s32[1,4]{1,0:T(1,128)} %len_ref.1) | copy-start | bytes 52

commit v2 on v1

--- a/solution.py
+++ b/solution.py
@@ -93,7 +93,9 @@
 
 
 MESH = pl.DeviceIdType.MESH
-CHUNKS = 2
+CHUNKS = 5
+EARLY = 3
+VMEM_LIMIT = 62 * 1024 * 1024
 
 
 def masked_attention(query, key_rows, value_rows, same, scaling):
@@ -116,21 +118,26 @@
 
 
 def layer_kernel(
-    n, groups, class_ref, len_ref, q_ref, k_ref, v_ref, w_ref, out_ref,
+    n, groups, class_hbm, len_hbm, q_hbm, k_hbm, v_hbm, w_ref, out_ref,
+    class_ref, len_ref, q_ref, k_ref, v_ref,
     packed, landed, spat, spat_in, tsend, temp_in, mixed, w_all,
     up_in, up_out, down_in, down_out,
-    qkv_s, qkv_r, w_s, w_r, w_l, sp_s, sp_r, sp_l, spf_s, t_s, t_r, t_l, tf_s,
+    load_s, qkv_s, qkv_r, w_s, w_r, w_l, sp_s, sp_r, share_s, share_r, t_s, t_r,
     up_s, up_r, down_s, down_r,
 ):
     pair = n // groups
     seq, head = lax.axis_index("seq"), lax.axis_index("head")
     plane, lane = seq // pair, lax.rem(seq, pair)
+    rank = lane * groups + head
     core = lax.rem(head, 2)
     sibling = head + 1 - 2 * core
+    across = lax.rem(head + groups // 2, groups)
+    at_home = plane == head
     tok, columns = q_ref.shape
     local_heads = columns // HD
-    width = tok // n
+    width, quarter = tok // n, tok // groups
     rows = w_ref.shape[0]
+    chunk = w_ref.shape[1] // CHUNKS
     scaling = 1.0 / math.sqrt(HD)
 
     def send(src, dst, send_sem, recv_sem, to_seq, to_head):
@@ -139,6 +146,14 @@
             device_id=(to_seq, to_head), device_id_type=MESH,
         )
 
+    loads = [
+        pltpu.make_async_copy(src, dst, load_s.at[i])
+        for i, (src, dst) in enumerate(
+            ((class_hbm, class_ref), (q_hbm, q_ref), (k_hbm, k_ref), (v_hbm, v_ref), (len_hbm, len_ref))
+        )
+    ]
+    for load in loads:
+        load.start()
     own_w = pltpu.make_async_copy(w_ref, w_all.at[lane], w_l)
     own_w.start()
 
@@ -148,13 +163,22 @@
         pl.semaphore_signal(barrier, inc=1, device_id=(to_seq, to_head), device_id_type=MESH)
 
     for step in range(1, n):
-        greet(lax.rem(seq + step, n), head)
-    greet(seq, sibling)
-
-    @pl.when(plane != head)
-    def _():
-        for peer in range(n):
-            greet(jnp.int32(peer), plane)
+        other = lax.rem(rank + step, n)
+        greet(plane * pair + other // groups, lax.rem(other, groups))
+    for step in range(1, groups):
+        for x in range(pair):
+            greet(lax.rem(plane + step, groups) * pair + x, plane)
+
+    @pl.when(plane > 0)
+    def _():
+        greet(seq - pair, head)
+
+    @pl.when(plane < groups - 1)
+    def _():
+        greet(seq + pair, head)
+
+    for load in loads[:4]:
+        load.wait()
 
     taken = slot_conditions(class_ref, head * local_heads, local_heads)
     for a, ref in enumerate((q_ref, k_ref, v_ref)):
@@ -173,19 +197,38 @@
     def _():
         down_in[...] = jnp.zeros_like(down_in)
 
-    pl.semaphore_wait(barrier, (n - 1) + pair * (groups - 1) + 1)
-
-    qkv = []
+    greeted = n - 1 + (plane > 0).astype(jnp.int32) + (plane < groups - 1).astype(jnp.int32)
+    pl.semaphore_wait(barrier, greeted + n * jnp.logical_not(at_home).astype(jnp.int32))
+
+    def qkv_copy(step):
+        to = lax.rem(rank + step, n)
+        return send(
+            packed.at[to], landed.at[seq], qkv_s.at[to], qkv_r.at[seq],
+            head * pair + to // groups, lax.rem(to, groups),
+        )
+
     for step in range(1, n):
-        peer = lax.rem(seq + step, n)
-        copy = send(packed.at[peer], landed.at[seq], qkv_s.at[peer], qkv_r.at[seq], peer, head)
-        copy.start()
-        qkv.append(copy)
-    landed[seq] = packed[seq]
-
-    other = plane * pair + (1 - lane)
-    w_copy = send(w_ref, w_all.at[lane], w_s, w_r.at[lane], other, head)
-    w_copy.start()
+        qkv_copy(step).start()
+
+    @pl.when(jnp.logical_not(at_home))
+    def _():
+        qkv_copy(0).start()
+
+    @pl.when(at_home)
+    def _():
+        landed[seq] = packed[rank]
+
+    def w_copy(c, owner):
+        cols = pl.ds(c * chunk, chunk)
+        return send(
+            w_ref.at[:, cols], w_all.at[owner, :, cols], w_s.at[c], w_r.at[c],
+            plane * pair + (1 - lane), head,
+        )
+
+    for c in range(EARLY):
+        w_copy(c, lane).start()
+
+    loads[4].wait()
 
     def window_of(axis):
         position = lax.broadcasted_iota(jnp.int32, (tok, tok), axis)
@@ -199,27 +242,46 @@
     same_window = window_of(0) == window_of(1)
     for h in range(local_heads):
         at = slice(h * HD, (h + 1) * HD)
-        spat[:, at] = masked_attention(q_ref[:, at], k_ref[:, at], v_ref[:, at], same_window, scaling)
-
-    sp_core = lax.rem(plane, 2)
-    sp_copies = []
-    for y in range(groups // 2):
-        to_seq, to_head = head * pair + lane, 2 * y + sp_core
-        mine = (to_seq == seq) & (to_head == head)
-        copy = send(spat, spat_in.at[plane], sp_s.at[y], sp_r.at[plane], to_seq, to_head)
-        sp_copies.append((mine, copy))
-
-        @pl.when(jnp.logical_not(mine))
-        def _(copy=copy):
-            copy.start()
-
-        @pl.when(mine)
-        def _():
-            spat_in[plane] = spat[...]
-
-    for step in range(1, n):
-        peer = lax.rem(seq + n - step, n)
-        send(landed.at[peer], landed.at[peer], qkv_s.at[peer], qkv_r.at[peer], peer, head).wait_recv()
+        value = masked_attention(q_ref[:, at], k_ref[:, at], v_ref[:, at], same_window, scaling)
+        spat[:, :, at] = value.reshape(groups, quarter, HD)
+
+    def spatial_copy(step):
+        to = lax.rem(head + step, groups)
+        return send(
+            spat.at[to], spat_in.at[to, plane], sp_s.at[to], sp_r.at[plane], head * pair + lane, to
+        )
+
+    for step in range(1, groups):
+        spatial_copy(step).start()
+
+    @pl.when(jnp.logical_not(at_home))
+    def _():
+        spatial_copy(0).start()
+
+    @pl.when(at_home)
+    def _():
+        spat_in[head, plane] = spat[head]
+
+    for source in range(n):
+        @pl.when(jnp.logical_not(at_home & (seq == source)))
+        def _(source=source):
+            send(
+                landed.at[source], landed.at[source], qkv_s.at[source], qkv_r.at[source], seq, head
+            ).wait_recv()
+
+    for z in range(groups):
+        @pl.when(jnp.logical_not(at_home & (plane == z)))
+        def _(z=z):
+            send(
+                spat.at[z], spat_in.at[head, z], sp_s.at[z], sp_r.at[z], seq, head
+            ).wait_recv()
+
+    def share(which, slot, to_head):
+        return send(spat_in.at[which], spat_in.at[which], share_s.at[slot], share_r.at[which], seq, to_head)
+
+    share(head, 0, across).start()
+    share(head, 1, sibling).start()
+
     row = lax.rem(lax.broadcasted_iota(jnp.int32, (tok, tok), 0), width)
     column = lax.rem(lax.broadcasted_iota(jnp.int32, (tok, tok), 1), width)
     same_position = row == column
@@ -232,66 +294,39 @@
         for f in range(n):
             tsend[f % pair, f // pair, :, t * HD:(t + 1) * HD] = result[f * width:(f + 1) * width]
 
-    t_core = lax.rem(seq, 2)
-    t_copies = []
-    for x in range(pair):
-        for y in range(groups // 2):
-            to_seq, to_head = head * pair + x, 2 * y + t_core
-            mine = (to_seq == seq) & (to_head == head)
-            copy = send(tsend.at[x], temp_in.at[seq], t_s.at[x, y], t_r.at[seq], to_seq, to_head)
-            t_copies.append((mine, copy))
-
-            @pl.when(jnp.logical_not(mine))
-            def _(copy=copy):
-                copy.start()
-
-            @pl.when(mine)
-            def _(x=x):
-                temp_in[seq] = tsend[x]
-
-    forwards = []
-    for j in range(groups // 2):
-        source = 2 * j + core
-        here = (source == plane) & (plane == head)
-        copy = send(spat_in.at[source], spat_in.at[source], spf_s.at[j], sp_r.at[source], seq, sibling)
-
-        @pl.when(jnp.logical_not(here))
-        def _(copy=copy):
-            copy.wait_recv()
-
-        copy.start()
-        forwards.append(copy)
-    for j in range(n // 2):
-        source = 2 * j + core
-        here = (source == seq) & (plane == head)
-        copy = send(temp_in.at[source], temp_in.at[source], tf_s.at[j], t_r.at[source], seq, sibling)
-
-        @pl.when(jnp.logical_not(here))
-        def _(copy=copy):
-            copy.wait_recv()
-
-        copy.start()
-        forwards.append(copy)
-    for j in range(groups // 2):
-        source = 2 * j + 1 - core
-        send(spat_in.at[source], spat_in.at[source], spf_s.at[j], sp_r.at[source], seq, sibling).wait_recv()
-    for j in range(n // 2):
-        source = 2 * j + 1 - core
-        send(temp_in.at[source], temp_in.at[source], tf_s.at[j], t_r.at[source], seq, sibling).wait_recv()
+    def temporal_copy(step):
+        to = lax.rem(rank + step, n)
+        x = to // groups
+        return send(
+            tsend.at[x], temp_in.at[rank], t_s.at[to], t_r.at[rank], plane * pair + x, lax.rem(to, groups)
+        )
+
+    for step in range(1, n):
+        temporal_copy(step).start()
+    temp_in[rank] = tsend[lane]
+    for c in range(EARLY, CHUNKS):
+        w_copy(c, lane).start()
+
+    share(across, 0, across).wait_recv()
+    share(across, 2, sibling).start()
+    share(sibling, 1, sibling).wait_recv()
+    share(lax.rem(sibling + groups // 2, groups), 2, sibling).wait_recv()
+    for step in range(1, n):
+        source = lax.rem(rank + n - step, n)
+        send(
+            temp_in.at[source], temp_in.at[source], t_s.at[source], t_r.at[source], seq, head
+        ).wait_recv()
 
     taken = slot_conditions(class_ref, plane * local_heads, local_heads)
     for z in range(groups):
         for h in range(local_heads):
-            value = spat_in[z, :, h * HD:(h + 1) * HD]
+            value = spat_in[:, z, :, h * HD:(h + 1) * HD].reshape(tok, HD)
             for t in range(min(h + 1, TMAX)):
                 slot = temp_in[:, z, :, t * HD:(t + 1) * HD].reshape(tok, HD)
                 value = jnp.where(taken[h][t], slot, value)
             mixed[z, :, h * HD:(h + 1) * HD] = value
 
     own_w.wait()
-    send(w_ref, w_all.at[1 - lane], w_s, w_r.at[1 - lane], other, head).wait_recv()
-
-    chunk = w_ref.shape[1] // CHUNKS
 
     def product(z, c):
         weight = w_all[:, :, c * chunk:(c + 1) * chunk].reshape(pair * rows, chunk)
@@ -316,8 +351,9 @@
             sign, came, goes, s_sem, r_sem = way
             send(goes.at[d, c], came.at[d, c], s_sem.at[d, c], r_sem.at[d, c], seq, head).wait_recv()
 
-    for d in range(groups - 1, 0, -1):
-        for c in range(CHUNKS):
+    for c in range(CHUNKS):
+        w_copy(c, 1 - lane).wait_recv()
+        for d in range(groups - 1, 0, -1):
             for way in ways:
                 @pl.when(reaches(way, d))
                 def _(way=way, d=d, c=c):
@@ -334,15 +370,21 @@
             total = total + way[1][0, c].astype(jnp.float32)
         out_ref[:, c * chunk:(c + 1) * chunk] = total.astype(jnp.bfloat16)
 
-    for copy in qkv:
-        copy.wait_send()
-    w_copy.wait_send()
-    for mine, copy in sp_copies + t_copies:
-        @pl.when(jnp.logical_not(mine))
-        def _(copy=copy):
-            copy.wait_send()
-    for copy in forwards:
-        copy.wait_send()
+    @pl.when(jnp.logical_not(at_home))
+    def _():
+        qkv_copy(0).wait_send()
+        spatial_copy(0).wait_send()
+
+    for step in range(1, n):
+        qkv_copy(step).wait_send()
+        temporal_copy(step).wait_send()
+    for step in range(1, groups):
+        spatial_copy(step).wait_send()
+    share(head, 0, across).wait_send()
+    share(head, 1, sibling).wait_send()
+    share(across, 2, sibling).wait_send()
+    for c in range(CHUNKS):
+        w_copy(c, lane).wait_send()
     for d in range(groups - 1, 0, -1):
         for c in range(CHUNKS):
             for way in ways:
@@ -354,22 +396,25 @@
 def kernel_body(n, groups, queries, keys, values, head_class, window_lengths, out_weight):
     tok, columns = queries.shape
     rows, out_columns = out_weight.shape
-    pair, width = n // groups, tok // n
+    pair, width, quarter = n // groups, tok // n, tok // groups
     chunk = out_columns // CHUNKS
     bf16, dma = jnp.bfloat16, pltpu.SemaphoreType.DMA
-    vmem = pl.BlockSpec(memory_space=pltpu.VMEM)
-    smem = pl.BlockSpec(memory_space=pltpu.SMEM)
     line = (groups - 1, CHUNKS)
     return pl.pallas_call(
         functools.partial(layer_kernel, n, groups),
         out_shape=jax.ShapeDtypeStruct((tok, out_columns), bf16),
-        in_specs=[smem, smem, vmem, vmem, vmem, pl.BlockSpec(memory_space=pl.ANY)],
-        out_specs=vmem,
+        in_specs=[pl.BlockSpec(memory_space=pl.ANY)] * 6,
+        out_specs=pl.BlockSpec(memory_space=pltpu.VMEM),
         scratch_shapes=[
+            pltpu.SMEM(head_class.shape, jnp.int32),
+            pltpu.SMEM(window_lengths.shape, jnp.int32),
+            pltpu.VMEM((tok, columns), bf16),
+            pltpu.VMEM((tok, columns), bf16),
+            pltpu.VMEM((tok, columns), bf16),
             pltpu.VMEM((n, width, 3 * TMAX * HD), bf16),
             pltpu.VMEM((n, width, 3 * TMAX * HD), bf16),
-            pltpu.VMEM((tok, columns), bf16),
-            pltpu.VMEM((groups, tok, columns), bf16),
+            pltpu.VMEM((groups, quarter, columns), bf16),
+            pltpu.VMEM((groups, groups, quarter, columns), bf16),
             pltpu.VMEM((pair, groups, width, TMAX * HD), bf16),
             pltpu.VMEM((n, groups, width, TMAX * HD), bf16),
             pltpu.VMEM((groups, tok, columns), bf16),
@@ -378,14 +423,14 @@
             pltpu.VMEM(line + (tok, chunk), bf16),
             pltpu.VMEM(line + (tok, chunk), bf16),
             pltpu.VMEM(line + (tok, chunk), bf16),
+            dma((5,)), dma((n,)), dma((n,)),
+            dma((CHUNKS,)), dma((CHUNKS,)), dma,
+            dma((groups,)), dma((groups,)), dma((3,)), dma((groups,)),
             dma((n,)), dma((n,)),
-            dma, dma((pair,)), dma,
-            dma((groups // 2,)), dma((groups,)), dma, dma((groups // 2,)),
-            dma((pair, groups // 2)), dma((n,)), dma, dma((n // 2,)),
             dma(line), dma(line), dma(line), dma(line),
         ],
         compiler_params=pltpu.CompilerParams(
-            collective_id=0, has_side_effects=True, vmem_limit_bytes=32 * 1024 * 1024
+            collective_id=0, has_side_effects=True, vmem_limit_bytes=VMEM_LIMIT
         ),
         cost_estimate=pl.CostEstimate(
             flops=2 * groups * tok * columns * out_columns,

time: 66.1 us -> 69.6 us (1.053); the launches traced: 64.9 us -> 69.4 us
  Pallas kernels: 59 us -> 67.7 us
  local copies, waits for them, and re-layouts: 5.93 us -> 1.72 us
    pallas_call x1, Pallas kernels: 59 us -> 67.7 us  [kernel_body(): pl.pallas_call(functools.partial(layer_kernel, n, groups), out_shape=jax....]
    unnamed x13 -> x1, local copies, waits for them, and re-layouts: 5.93 us -> 1.72 us
where the time goes in v2:
time: 69.6 us; the launch traced here: 69.4 us
  Pallas kernels  67.7 us (97%)
  local copies, waits for them, and re-layouts  1.72 us (2%)
    pallas_call x1, Pallas kernels, kernel_body(): pl.pallas_call(functools.partial(layer_kernel, n, groups), out_shape=jax....  67.7 us
    unnamed x1, local copies, waits for them, and re-layouts  1.72 us

profile of v2, /device:TPU:0, one launch (start us, length us, event | category | flops | bytes accessed | tf_op | source)
XLA Modules:
  0.0 69.4 jit_solution(5049916401839048672)
XLA Ops:
  0.0 67.7 %shard_map.64 = bf16[128,1280]{1,0:T(8,128)(2,1)} custom-call(s32[20]{0:T(128)} %class_hbm.1, s32[1,4]{1,0:T(1,128)} %len_hbm.1, bf16[128,640]{1,0:T(8,128)(2,1)} %q_hbm.1, bf16[128,640]{1,0:T(8,128)(2,1)} %k_hbm.1, bf16[128,640]{1,0:T(8,128)(2,1)} %v_hbm.1, bf16[320,1280]{1,0:T(8,128)(2,1)} %w_ref.1), custom_call_target="tpu_custom_call" | custom-call | flops 838860800 | bytes 1638400 | tf_op jit(solution)/shard_map/pallas_call | solution.py:403
  67.7 1.7 %copy.8 = bf16[128,1280]{1,0:T(8,128)(2,1)} copy(bf16[128,1280]{1,0:T(8,128)(2,1)} %shard_map.64) | data formatting | bytes 655360

commit v3 on v2

--- a/solution.py
+++ b/solution.py
@@ -94,17 +94,24 @@
 
 MESH = pl.DeviceIdType.MESH
 CHUNKS = 5
-EARLY = 3
+EARLY = 2
 VMEM_LIMIT = 62 * 1024 * 1024
 
 
-def masked_attention(query, key_rows, value_rows, same, scaling):
-    scores = lax.dot_general(
-        query, key_rows, (((1,), (1,)), ((), ())), preferred_element_type=jnp.float32
-    )
-    scores = jnp.where(same, scores * scaling, -1e30)
-    weights = softmax_rows(scores).astype(jnp.bfloat16)
-    return jnp.dot(weights, value_rows, preferred_element_type=jnp.float32).astype(jnp.bfloat16)
+def masked_attention(triples, same, scaling):
+    scores = [
+        lax.dot_general(q, k, (((1,), (1,)), ((), ())), preferred_element_type=jnp.float32)
+        for q, k, _ in triples
+    ]
+    scores = [jnp.where(same, score * scaling, -1e30) for score in scores]
+    highest = [jnp.max(score, axis=-1, keepdims=True) for score in scores]
+    weights = [jnp.exp(score - top) for score, top in zip(scores, highest)]
+    totals = [jnp.sum(weight, axis=-1, keepdims=True) for weight in weights]
+    weights = [(weight / total).astype(jnp.bfloat16) for weight, total in zip(weights, totals)]
+    return [
+        jnp.dot(weight, v, preferred_element_type=jnp.float32).astype(jnp.bfloat16)
+        for weight, (_, _, v) in zip(weights, triples)
+    ]
 
 
 def slot_conditions(class_ref, first, local_heads):
@@ -120,7 +127,7 @@
 def layer_kernel(
     n, groups, class_hbm, len_hbm, q_hbm, k_hbm, v_hbm, w_ref, out_ref,
     class_ref, len_ref, q_ref, k_ref, v_ref,
-    packed, landed, spat, spat_in, tsend, temp_in, mixed, w_all,
+    packed, landed, spat, spat_in, tsend, temp_in, mixed, w_all, partial,
     up_in, up_out, down_in, down_out,
     load_s, qkv_s, qkv_r, w_s, w_r, w_l, sp_s, sp_r, share_s, share_r, t_s, t_r,
     up_s, up_r, down_s, down_r,
@@ -240,9 +247,11 @@
         return ids
 
     same_window = window_of(0) == window_of(1)
-    for h in range(local_heads):
-        at = slice(h * HD, (h + 1) * HD)
-        value = masked_attention(q_ref[:, at], k_ref[:, at], v_ref[:, at], same_window, scaling)
+    spans = [slice(h * HD, (h + 1) * HD) for h in range(local_heads)]
+    results = masked_attention(
+        [(q_ref[:, at], k_ref[:, at], v_ref[:, at]) for at in spans], same_window, scaling
+    )
+    for at, value in zip(spans, results):
         spat[:, :, at] = value.reshape(groups, quarter, HD)
 
     def spatial_copy(step):
@@ -285,12 +294,14 @@
     row = lax.rem(lax.broadcasted_iota(jnp.int32, (tok, tok), 0), width)
     column = lax.rem(lax.broadcasted_iota(jnp.int32, (tok, tok), 1), width)
     same_position = row == column
-    for t in range(TMAX):
-        query, key_rows, value_rows = (
+    triples = [
+        tuple(
             landed[:, :, (a * TMAX + t) * HD:(a * TMAX + t + 1) * HD].reshape(tok, HD)
             for a in range(3)
         )
-        result = masked_attention(query, key_rows, value_rows, same_position, scaling)
+        for t in range(TMAX)
+    ]
+    for t, result in enumerate(masked_attention(triples, same_position, scaling)):
         for f in range(n):
             tsend[f % pair, f // pair, :, t * HD:(t + 1) * HD] = result[f * width:(f + 1) * width]
 
@@ -328,9 +339,13 @@
 
     own_w.wait()
 
-    def product(z, c):
+    def multiply(c):
+        w_copy(c, 1 - lane).wait_recv()
         weight = w_all[:, :, c * chunk:(c + 1) * chunk].reshape(pair * rows, chunk)
-        return jnp.dot(mixed[z], weight, preferred_element_type=jnp.float32)
+        result = jnp.dot(
+            mixed[...].reshape(groups * tok, columns), weight, preferred_element_type=jnp.float32
+        )
+        partial[c] = result.reshape(groups, tok, chunk)
 
     ways = ((1, up_in, up_out, up_s, up_r), (-1, down_in, down_out, down_s, down_r))
 
@@ -352,19 +367,19 @@
             send(goes.at[d, c], came.at[d, c], s_sem.at[d, c], r_sem.at[d, c], seq, head).wait_recv()
 
     for c in range(CHUNKS):
-        w_copy(c, 1 - lane).wait_recv()
+        multiply(c)
         for d in range(groups - 1, 0, -1):
             for way in ways:
                 @pl.when(reaches(way, d))
                 def _(way=way, d=d, c=c):
-                    total = product(plane + way[0] * d, c)
+                    total = partial[c, plane + way[0] * d]
                     if d < groups - 1:
                         arrive(way, d, c)
                         total = total + way[1][d, c].astype(jnp.float32)
                     way[2][d - 1, c] = total.astype(jnp.bfloat16)
                     onward(way, d, c).start()
     for c in range(CHUNKS):
-        total = product(plane, c)
+        total = partial[c, plane]
         for way in ways:
             arrive(way, 0, c)
             total = total + way[1][0, c].astype(jnp.float32)
@@ -419,6 +434,7 @@
             pltpu.VMEM((n, groups, width, TMAX * HD), bf16),
             pltpu.VMEM((groups, tok, columns), bf16),
             pltpu.VMEM((pair, rows, out_columns), bf16),
+            pltpu.VMEM((CHUNKS, groups, tok, chunk), jnp.float32),
             pltpu.VMEM(line + (tok, chunk), bf16),
             pltpu.VMEM(line + (tok, chunk), bf16),
             pltpu.VMEM(line + (tok, chunk), bf16),

time: 69.6 us -> 69.1 us (level)
  no operation moved by 1% of the time
where the time goes in v3:
time: 69.1 us; the launch traced here: 69 us
  Pallas kernels  67.2 us (97%)
  local copies, waits for them, and re-layouts  1.72 us (2%)
    pallas_call x1, Pallas kernels, kernel_body(): pl.pallas_call(functools.partial(layer_kernel, n, groups), out_shape=jax....  67.2 us
    unnamed x1, local copies, waits for them, and re-layouts  1.72 us

profile of v3, /device:TPU:0, one launch (start us, length us, event | category | flops | bytes accessed | tf_op | source)
XLA Modules:
  0.0 69.0 jit_solution(18341511200406311485)
XLA Ops:
  0.0 67.2 %shard_map.64 = bf16[128,1280]{1,0:T(8,128)(2,1)} custom-call(s32[20]{0:T(128)} %class_hbm.1, s32[1,4]{1,0:T(1,128)} %len_hbm.1, bf16[128,640]{1,0:T(8,128)(2,1)} %q_hbm.1, bf16[128,640]{1,0:T(8,128)(2,1)} %k_hbm.1, bf16[128,640]{1,0:T(8,128)(2,1)} %v_hbm.1, bf16[320,1280]{1,0:T(8,128)(2,1)} %w_ref.1), custom_call_target="tpu_custom_call" | custom-call | flops 838860800 | bytes 1638400 | tf_op jit(solution)/shard_map/pallas_call | solution.py:418
  67.2 1.7 %copy.8 = bf16[128,1280]{1,0:T(8,128)(2,1)} copy(bf16[128,1280]{1,0:T(8,128)(2,1)} %shard_map.64) | data formatting | bytes 655360

commit v4 on v1

--- a/solution.py
+++ b/solution.py
@@ -94,15 +94,23 @@
 
 MESH = pl.DeviceIdType.MESH
 CHUNKS = 2
-
-
-def masked_attention(query, key_rows, value_rows, same, scaling):
-    scores = lax.dot_general(
-        query, key_rows, (((1,), (1,)), ((), ())), preferred_element_type=jnp.float32
-    )
-    scores = jnp.where(same, scores * scaling, -1e30)
-    weights = softmax_rows(scores).astype(jnp.bfloat16)
-    return jnp.dot(weights, value_rows, preferred_element_type=jnp.float32).astype(jnp.bfloat16)
+VMEM_LIMIT = 62 * 1024 * 1024
+
+
+def masked_attention(triples, same, scaling):
+    scores = [
+        lax.dot_general(q, k, (((1,), (1,)), ((), ())), preferred_element_type=jnp.float32)
+        for q, k, _ in triples
+    ]
+    scores = [jnp.where(same, score * scaling, -1e30) for score in scores]
+    highest = [jnp.max(score, axis=-1, keepdims=True) for score in scores]
+    weights = [jnp.exp(score - top) for score, top in zip(scores, highest)]
+    totals = [jnp.sum(weight, axis=-1, keepdims=True) for weight in weights]
+    weights = [(weight / total).astype(jnp.bfloat16) for weight, total in zip(weights, totals)]
+    return [
+        jnp.dot(weight, v, preferred_element_type=jnp.float32).astype(jnp.bfloat16)
+        for weight, (_, _, v) in zip(weights, triples)
+    ]
 
 
 def slot_conditions(class_ref, first, local_heads):
@@ -116,10 +124,11 @@
 
 
 def layer_kernel(
-    n, groups, class_ref, len_ref, q_ref, k_ref, v_ref, w_ref, out_ref,
-    packed, landed, spat, spat_in, tsend, temp_in, mixed, w_all,
+    n, groups, class_hbm, len_hbm, q_hbm, k_hbm, v_hbm, w_ref, out_ref,
+    class_ref, len_ref, q_ref, k_ref, v_ref,
+    packed, landed, spat, spat_in, tsend, temp_in, mixed, w_all, partial,
     up_in, up_out, down_in, down_out,
-    qkv_s, qkv_r, w_s, w_r, w_l, sp_s, sp_r, sp_l, spf_s, t_s, t_r, t_l, tf_s,
+    load_s, qkv_s, qkv_r, w_s, w_r, w_l, sp_s, sp_r, sp_l, spf_s, t_s, t_r, t_l, tf_s,
     up_s, up_r, down_s, down_r,
 ):
     pair = n // groups
@@ -139,6 +148,14 @@
             device_id=(to_seq, to_head), device_id_type=MESH,
         )
 
+    loads = [
+        pltpu.make_async_copy(src, dst, load_s.at[i])
+        for i, (src, dst) in enumerate(
+            ((class_hbm, class_ref), (q_hbm, q_ref), (k_hbm, k_ref), (v_hbm, v_ref), (len_hbm, len_ref))
+        )
+    ]
+    for load in loads:
+        load.start()
     own_w = pltpu.make_async_copy(w_ref, w_all.at[lane], w_l)
     own_w.start()
 
@@ -155,6 +172,9 @@
     def _():
         for peer in range(n):
             greet(jnp.int32(peer), plane)
+
+    for load in loads[:4]:
+        load.wait()
 
     taken = slot_conditions(class_ref, head * local_heads, local_heads)
     for a, ref in enumerate((q_ref, k_ref, v_ref)):
@@ -187,6 +207,7 @@
     w_copy = send(w_ref, w_all.at[lane], w_s, w_r.at[lane], other, head)
     w_copy.start()
 
+    loads[4].wait()
     def window_of(axis):
         position = lax.broadcasted_iota(jnp.int32, (tok, tok), axis)
         ids = jnp.zeros((tok, tok), jnp.int32)
@@ -197,9 +218,12 @@
         return ids
 
     same_window = window_of(0) == window_of(1)
-    for h in range(local_heads):
-        at = slice(h * HD, (h + 1) * HD)
-        spat[:, at] = masked_attention(q_ref[:, at], k_ref[:, at], v_ref[:, at], same_window, scaling)
+    spans = [slice(h * HD, (h + 1) * HD) for h in range(local_heads)]
+    results = masked_attention(
+        [(q_ref[:, at], k_ref[:, at], v_ref[:, at]) for at in spans], same_window, scaling
+    )
+    for at, value in zip(spans, results):
+        spat[:, at] = value
 
     sp_core = lax.rem(plane, 2)
     sp_copies = []
@@ -223,12 +247,14 @@
     row = lax.rem(lax.broadcasted_iota(jnp.int32, (tok, tok), 0), width)
     column = lax.rem(lax.broadcasted_iota(jnp.int32, (tok, tok), 1), width)
     same_position = row == column
-    for t in range(TMAX):
-        query, key_rows, value_rows = (
+    triples = [
+        tuple(
             landed[:, :, (a * TMAX + t) * HD:(a * TMAX + t + 1) * HD].reshape(tok, HD)
             for a in range(3)
         )
-        result = masked_attention(query, key_rows, value_rows, same_position, scaling)
+        for t in range(TMAX)
+    ]
+    for t, result in enumerate(masked_attention(triples, same_position, scaling)):
         for f in range(n):
             tsend[f % pair, f // pair, :, t * HD:(t + 1) * HD] = result[f * width:(f + 1) * width]
 
@@ -293,9 +319,12 @@
 
     chunk = w_ref.shape[1] // CHUNKS
 
-    def product(z, c):
+    def multiply(c):
         weight = w_all[:, :, c * chunk:(c + 1) * chunk].reshape(pair * rows, chunk)
-        return jnp.dot(mixed[z], weight, preferred_element_type=jnp.float32)
+        result = jnp.dot(
+            mixed[...].reshape(groups * tok, columns), weight, preferred_element_type=jnp.float32
+        )
+        partial[c] = result.reshape(groups, tok, chunk)
 
     ways = ((1, up_in, up_out, up_s, up_r), (-1, down_in, down_out, down_s, down_r))
 
@@ -318,17 +347,19 @@
 
     for d in range(groups - 1, 0, -1):
         for c in range(CHUNKS):
+            if d == groups - 1:
+                multiply(c)
             for way in ways:
                 @pl.when(reaches(way, d))
                 def _(way=way, d=d, c=c):
-                    total = product(plane + way[0] * d, c)
+                    total = partial[c, plane + way[0] * d]
                     if d < groups - 1:
                         arrive(way, d, c)
                         total = total + way[1][d, c].astype(jnp.float32)
                     way[2][d - 1, c] = total.astype(jnp.bfloat16)
                     onward(way, d, c).start()
     for c in range(CHUNKS):
-        total = product(plane, c)
+        total = partial[c, plane]
         for way in ways:
             arrive(way, 0, c)
             total = total + way[1][0, c].astype(jnp.float32)
@@ -357,15 +388,18 @@
     pair, width = n // groups, tok // n
     chunk = out_columns // CHUNKS
     bf16, dma = jnp.bfloat16, pltpu.SemaphoreType.DMA
-    vmem = pl.BlockSpec(memory_space=pltpu.VMEM)
-    smem = pl.BlockSpec(memory_space=pltpu.SMEM)
     line = (groups - 1, CHUNKS)
     return pl.pallas_call(
         functools.partial(layer_kernel, n, groups),
         out_shape=jax.ShapeDtypeStruct((tok, out_columns), bf16),
-        in_specs=[smem, smem, vmem, vmem, vmem, pl.BlockSpec(memory_space=pl.ANY)],
-        out_specs=vmem,
+        in_specs=[pl.BlockSpec(memory_space=pl.ANY)] * 6,
+        out_specs=pl.BlockSpec(memory_space=pltpu.VMEM),
         scratch_shapes=[
+            pltpu.SMEM(head_class.shape, jnp.int32),
+            pltpu.SMEM(window_lengths.shape, jnp.int32),
+            pltpu.VMEM((tok, columns), bf16),
+            pltpu.VMEM((tok, columns), bf16),
+            pltpu.VMEM((tok, columns), bf16),
             pltpu.VMEM((n, width, 3 * TMAX * HD), bf16),
             pltpu.VMEM((n, width, 3 * TMAX * HD), bf16),
             pltpu.VMEM((tok, columns), bf16),
@@ -374,18 +408,19 @@
             pltpu.VMEM((n, groups, width, TMAX * HD), bf16),
             pltpu.VMEM((groups, tok, columns), bf16),
             pltpu.VMEM((pair, rows, out_columns), bf16),
+            pltpu.VMEM((CHUNKS, groups, tok, chunk), jnp.float32),
             pltpu.VMEM(line + (tok, chunk), bf16),
             pltpu.VMEM(line + (tok, chunk), bf16),
             pltpu.VMEM(line + (tok, chunk), bf16),
             pltpu.VMEM(line + (tok, chunk), bf16),
-            dma((n,)), dma((n,)),
+            dma((5,)), dma((n,)), dma((n,)),
             dma, dma((pair,)), dma,
             dma((groups // 2,)), dma((groups,)), dma, dma((groups // 2,)),
             dma((pair, groups // 2)), dma((n,)), dma, dma((n // 2,)),
             dma(line), dma(line), dma(line), dma(line),
         ],
         compiler_params=pltpu.CompilerParams(
-            collective_id=0, has_side_effects=True, vmem_limit_bytes=32 * 1024 * 1024
+            collective_id=0, has_side_effects=True, vmem_limit_bytes=VMEM_LIMIT
         ),
         cost_estimate=pl.CostEstimate(
             flops=2 * groups * tok * columns * out_columns,

time: 66.1 us -> 62.2 us (0.941)
  the two profiles are of different devices: /device:TPU:0 before, /device:TPU:15 now
where the time goes in v4:
time: 62.2 us; the launch traced here: 62 us
  Pallas kernels  60.3 us (97%)
  local copies, waits for them, and re-layouts  1.72 us (3%)
    pallas_call x1, Pallas kernels, kernel_body(): pl.pallas_call(functools.partial(layer_kernel, n, groups), out_shape=jax....  60.3 us
    unnamed x1, local copies, waits for them, and re-layouts  1.72 us

profile of v4, /device:TPU:15, one launch (start us, length us, event | category | flops | bytes accessed | tf_op | source)
XLA Modules:
  0.0 62.0 jit_solution(17256970966342345252)
XLA Ops:
  0.0 60.3 %shard_map.64 = bf16[128,1280]{1,0:T(8,128)(2,1)} custom-call(s32[20]{0:T(128)} %class_hbm.1, s32[1,4]{1,0:T(1,128)} %len_hbm.1, bf16[128,640]{1,0:T(8,128)(2,1)} %q_hbm.1, bf16[128,640]{1,0:T(8,128)(2,1)} %k_hbm.1, bf16[128,640]{1,0:T(8,128)(2,1)} %v_hbm.1, bf16[320,1280]{1,0:T(8,128)(2,1)} %w_ref.1), custom_call_target="tpu_custom_call" | custom-call | flops 838860800 | bytes 1638400 | tf_op jit(solution)/shard_map/pallas_call | solution.py:392
  60.3 1.7 %copy.8 = bf16[128,1280]{1,0:T(8,128)(2,1)} copy(bf16[128,1280]{1,0:T(8,128)(2,1)} %shard_map.64) | data formatting | bytes 655360

commit v5 on v4

--- a/solution.py
+++ b/solution.py
@@ -128,7 +128,7 @@
     class_ref, len_ref, q_ref, k_ref, v_ref,
     packed, landed, spat, spat_in, tsend, temp_in, mixed, w_all, partial,
     up_in, up_out, down_in, down_out,
-    load_s, qkv_s, qkv_r, w_s, w_r, w_l, sp_s, sp_r, sp_l, spf_s, t_s, t_r, t_l, tf_s,
+    load_s, qkv_s, qkv_r, w_s, w_r, w_l, sp_s, sp_r, share_s, share_r, t_s, t_r, tf_s,
     up_s, up_r, down_s, down_r,
 ):
     pair = n // groups
@@ -136,9 +136,11 @@
     plane, lane = seq // pair, lax.rem(seq, pair)
     core = lax.rem(head, 2)
     sibling = head + 1 - 2 * core
+    across = lax.rem(head + groups // 2, groups)
     tok, columns = q_ref.shape
     local_heads = columns // HD
-    width = tok // n
+    width, quarter = tok // n, tok // groups
+    chunk = w_ref.shape[1] // CHUNKS
     rows = w_ref.shape[0]
     scaling = 1.0 / math.sqrt(HD)
 
@@ -167,6 +169,7 @@
     for step in range(1, n):
         greet(lax.rem(seq + step, n), head)
     greet(seq, sibling)
+    greet(seq, across)
 
     @pl.when(plane != head)
     def _():
@@ -193,7 +196,7 @@
     def _():
         down_in[...] = jnp.zeros_like(down_in)
 
-    pl.semaphore_wait(barrier, (n - 1) + pair * (groups - 1) + 1)
+    pl.semaphore_wait(barrier, (n - 1) + pair * (groups - 1) + 2)
 
     qkv = []
     for step in range(1, n):
@@ -204,8 +207,13 @@
     landed[seq] = packed[seq]
 
     other = plane * pair + (1 - lane)
-    w_copy = send(w_ref, w_all.at[lane], w_s, w_r.at[lane], other, head)
-    w_copy.start()
+
+    def w_copy(c, owner):
+        cols = pl.ds(c * chunk, chunk)
+        return send(w_ref.at[:, cols], w_all.at[owner, :, cols], w_s.at[c], w_r.at[c], other, head)
+
+    for c in range(CHUNKS):
+        w_copy(c, lane).start()
 
     loads[4].wait()
     def window_of(axis):
@@ -223,23 +231,26 @@
         [(q_ref[:, at], k_ref[:, at], v_ref[:, at]) for at in spans], same_window, scaling
     )
     for at, value in zip(spans, results):
-        spat[:, at] = value
-
-    sp_core = lax.rem(plane, 2)
-    sp_copies = []
-    for y in range(groups // 2):
-        to_seq, to_head = head * pair + lane, 2 * y + sp_core
-        mine = (to_seq == seq) & (to_head == head)
-        copy = send(spat, spat_in.at[plane], sp_s.at[y], sp_r.at[plane], to_seq, to_head)
-        sp_copies.append((mine, copy))
-
-        @pl.when(jnp.logical_not(mine))
-        def _(copy=copy):
-            copy.start()
-
-        @pl.when(mine)
-        def _():
-            spat_in[plane] = spat[...]
+        spat[:, :, at] = value.reshape(groups, quarter, HD)
+
+    at_home = plane == head
+
+    def spatial_copy(step):
+        to = lax.rem(head + step, groups)
+        return send(
+            spat.at[to], spat_in.at[to, plane], sp_s.at[to], sp_r.at[plane], head * pair + lane, to
+        )
+
+    for step in range(1, groups):
+        spatial_copy(step).start()
+
+    @pl.when(jnp.logical_not(at_home))
+    def _():
+        spatial_copy(0).start()
+
+    @pl.when(at_home)
+    def _():
+        spat_in[head, plane] = spat[head]
 
     for step in range(1, n):
         peer = lax.rem(seq + n - step, n)
@@ -275,18 +286,18 @@
             def _(x=x):
                 temp_in[seq] = tsend[x]
 
-    forwards = []
-    for j in range(groups // 2):
-        source = 2 * j + core
-        here = (source == plane) & (plane == head)
-        copy = send(spat_in.at[source], spat_in.at[source], spf_s.at[j], sp_r.at[source], seq, sibling)
-
-        @pl.when(jnp.logical_not(here))
-        def _(copy=copy):
-            copy.wait_recv()
-
-        copy.start()
-        forwards.append(copy)
+    def share(which, slot, to_head):
+        return send(spat_in.at[which], spat_in.at[which], share_s.at[slot], share_r.at[which], seq, to_head)
+
+    for z in range(groups):
+        @pl.when(jnp.logical_not(at_home & (plane == z)))
+        def _(z=z):
+            send(spat.at[z], spat_in.at[head, z], sp_s.at[z], sp_r.at[z], seq, head).wait_recv()
+
+    share(head, 0, across).start()
+    share(head, 1, sibling).start()
+
+    forwards = [share(head, 0, across), share(head, 1, sibling), share(across, 2, sibling)]
     for j in range(n // 2):
         source = 2 * j + core
         here = (source == seq) & (plane == head)
@@ -298,9 +309,10 @@
 
         copy.start()
         forwards.append(copy)
-    for j in range(groups // 2):
-        source = 2 * j + 1 - core
-        send(spat_in.at[source], spat_in.at[source], spf_s.at[j], sp_r.at[source], seq, sibling).wait_recv()
+    share(across, 0, across).wait_recv()
+    share(across, 2, sibling).start()
+    share(sibling, 1, sibling).wait_recv()
+    share(lax.rem(sibling + groups // 2, groups), 2, sibling).wait_recv()
     for j in range(n // 2):
         source = 2 * j + 1 - core
         send(temp_in.at[source], temp_in.at[source], tf_s.at[j], t_r.at[source], seq, sibling).wait_recv()
@@ -308,18 +320,16 @@
     taken = slot_conditions(class_ref, plane * local_heads, local_heads)
     for z in range(groups):
         for h in range(local_heads):
-            value = spat_in[z, :, h * HD:(h + 1) * HD]
+            value = spat_in[:, z, :, h * HD:(h + 1) * HD].reshape(tok, HD)
             for t in range(min(h + 1, TMAX)):
                 slot = temp_in[:, z, :, t * HD:(t + 1) * HD].reshape(tok, HD)
                 value = jnp.where(taken[h][t], slot, value)
             mixed[z, :, h * HD:(h + 1) * HD] = value
 
     own_w.wait()
-    send(w_ref, w_all.at[1 - lane], w_s, w_r.at[1 - lane], other, head).wait_recv()
-
-    chunk = w_ref.shape[1] // CHUNKS
 
     def multiply(c):
+        w_copy(c, 1 - lane).wait_recv()
         weight = w_all[:, :, c * chunk:(c + 1) * chunk].reshape(pair * rows, chunk)
         result = jnp.dot(
             mixed[...].reshape(groups * tok, columns), weight, preferred_element_type=jnp.float32
@@ -345,10 +355,9 @@
             sign, came, goes, s_sem, r_sem = way
             send(goes.at[d, c], came.at[d, c], s_sem.at[d, c], r_sem.at[d, c], seq, head).wait_recv()
 
-    for d in range(groups - 1, 0, -1):
-        for c in range(CHUNKS):
-            if d == groups - 1:
-                multiply(c)
+    for c in range(CHUNKS):
+        multiply(c)
+        for d in range(groups - 1, 0, -1):
             for way in ways:
                 @pl.when(reaches(way, d))
                 def _(way=way, d=d, c=c):
@@ -367,8 +376,16 @@
 
     for copy in qkv:
         copy.wait_send()
-    w_copy.wait_send()
-    for mine, copy in sp_copies + t_copies:
+    for c in range(CHUNKS):
+        w_copy(c, lane).wait_send()
+    for step in range(1, groups):
+        spatial_copy(step).wait_send()
+
+    @pl.when(jnp.logical_not(at_home))
+    def _():
+        spatial_copy(0).wait_send()
+
+    for mine, copy in t_copies:
         @pl.when(jnp.logical_not(mine))
         def _(copy=copy):
             copy.wait_send()
@@ -385,7 +402,7 @@
 def kernel_body(n, groups, queries, keys, values, head_class, window_lengths, out_weight):
     tok, columns = queries.shape
     rows, out_columns = out_weight.shape
-    pair, width = n // groups, tok // n
+    pair, width, quarter = n // groups, tok // n, tok // groups
     chunk = out_columns // CHUNKS
     bf16, dma = jnp.bfloat16, pltpu.SemaphoreType.DMA
     line = (groups - 1, CHUNKS)
@@ -402,8 +419,8 @@
             pltpu.VMEM((tok, columns), bf16),
             pltpu.VMEM((n, width, 3 * TMAX * HD), bf16),
             pltpu.VMEM((n, width, 3 * TMAX * HD), bf16),
-            pltpu.VMEM((tok, columns), bf16),
-            pltpu.VMEM((groups, tok, columns), bf16),
+            pltpu.VMEM((groups, quarter, columns), bf16),
+            pltpu.VMEM((groups, groups, quarter, columns), bf16),
             pltpu.VMEM((pair, groups, width, TMAX * HD), bf16),
             pltpu.VMEM((n, groups, width, TMAX * HD), bf16),
             pltpu.VMEM((groups, tok, columns), bf16),
@@ -414,9 +431,9 @@
             pltpu.VMEM(line + (tok, chunk), bf16),
             pltpu.VMEM(line + (tok, chunk), bf16),
             dma((5,)), dma((n,)), dma((n,)),
-            dma, dma((pair,)), dma,
-            dma((groups // 2,)), dma((groups,)), dma, dma((groups // 2,)),
-            dma((pair, groups // 2)), dma((n,)), dma, dma((n // 2,)),
+            dma((CHUNKS,)), dma((CHUNKS,)), dma,
+            dma((groups,)), dma((groups,)), dma((3,)), dma((groups,)),
+            dma((pair, groups // 2)), dma((n,)), dma((n // 2,)),
             dma(line), dma(line), dma(line), dma(line),
         ],
         compiler_params=pltpu.CompilerParams(

time: 62.2 us -> 63.6 us (1.023)
  the two profiles are of different devices: /device:TPU:15 before, /device:TPU:0 now
where the time goes in v5:
time: 63.6 us; the launch traced here: 63.4 us
  Pallas kernels  61.7 us (97%)
  local copies, waits for them, and re-layouts  1.72 us (3%)
    pallas_call x1, Pallas kernels, kernel_body(): pl.pallas_call(functools.partial(layer_kernel, n, groups), out_shape=jax....  61.7 us
    unnamed x1, local copies, waits for them, and re-layouts  1.72 us

profile of v5, /device:TPU:0, one launch (start us, length us, event | category | flops | bytes accessed | tf_op | source)
XLA Modules:
  0.0 63.4 jit_solution(17764079914179759611)
XLA Ops:
  0.0 61.7 %shard_map.64 = bf16[128,1280]{1,0:T(8,128)(2,1)} custom-call(s32[20]{0:T(128)} %class_hbm.1, s32[1,4]{1,0:T(1,128)} %len_hbm.1, bf16[128,640]{1,0:T(8,128)(2,1)} %q_hbm.1, bf16[128,640]{1,0:T(8,128)(2,1)} %k_hbm.1, bf16[128,640]{1,0:T(8,128)(2,1)} %v_hbm.1, bf16[320,1280]{1,0:T(8,128)(2,1)} %w_ref.1), custom_call_target="tpu_custom_call" | custom-call | flops 838860800 | bytes 1638400 | tf_op jit(solution)/shard_map/pallas_call | solution.py:409
  61.7 1.7 %copy.8 = bf16[128,1280]{1,0:T(8,128)(2,1)} copy(bf16[128,1280]{1,0:T(8,128)(2,1)} %shard_map.64) | data formatting | bytes 655360

commit v6 on v4

--- a/solution.py
+++ b/solution.py
@@ -139,6 +139,7 @@
     tok, columns = q_ref.shape
     local_heads = columns // HD
     width = tok // n
+    chunk = w_ref.shape[1] // CHUNKS
     rows = w_ref.shape[0]
     scaling = 1.0 / math.sqrt(HD)
 
@@ -204,8 +205,15 @@
     landed[seq] = packed[seq]
 
     other = plane * pair + (1 - lane)
-    w_copy = send(w_ref, w_all.at[lane], w_s, w_r.at[lane], other, head)
-    w_copy.start()
+
+    def w_copy(c, owner):
+        cols = pl.ds(c * chunk, chunk)
+        return send(w_ref.at[:, cols], w_all.at[owner, :, cols], w_s.at[c], w_r.at[c], other, head)
+
+    @pl.when(core == 0)
+    def _():
+        for c in range(CHUNKS):
+            w_copy(c, lane).start()
 
     loads[4].wait()
     def window_of(axis):
@@ -275,6 +283,10 @@
             def _(x=x):
                 temp_in[seq] = tsend[x]
 
+    @pl.when(core == 1)
+    def _():
+        w_copy(0, lane).start()
+
     forwards = []
     for j in range(groups // 2):
         source = 2 * j + core
@@ -298,6 +310,12 @@
 
         copy.start()
         forwards.append(copy)
+
+    @pl.when(core == 1)
+    def _():
+        for c in range(1, CHUNKS):
+            w_copy(c, lane).start()
+
     for j in range(groups // 2):
         source = 2 * j + 1 - core
         send(spat_in.at[source], spat_in.at[source], spf_s.at[j], sp_r.at[source], seq, sibling).wait_recv()
@@ -315,11 +333,9 @@
             mixed[z, :, h * HD:(h + 1) * HD] = value
 
     own_w.wait()
-    send(w_ref, w_all.at[1 - lane], w_s, w_r.at[1 - lane], other, head).wait_recv()
-
-    chunk = w_ref.shape[1] // CHUNKS
 
     def multiply(c):
+        w_copy(c, 1 - lane).wait_recv()
         weight = w_all[:, :, c * chunk:(c + 1) * chunk].reshape(pair * rows, chunk)
         result = jnp.dot(
             mixed[...].reshape(groups * tok, columns), weight, preferred_element_type=jnp.float32
@@ -345,10 +361,9 @@
             sign, came, goes, s_sem, r_sem = way
             send(goes.at[d, c], came.at[d, c], s_sem.at[d, c], r_sem.at[d, c], seq, head).wait_recv()
 
-    for d in range(groups - 1, 0, -1):
-        for c in range(CHUNKS):
-            if d == groups - 1:
-                multiply(c)
+    for c in range(CHUNKS):
+        multiply(c)
+        for d in range(groups - 1, 0, -1):
             for way in ways:
                 @pl.when(reaches(way, d))
                 def _(way=way, d=d, c=c):
@@ -367,7 +382,8 @@
 
     for copy in qkv:
         copy.wait_send()
-    w_copy.wait_send()
+    for c in range(CHUNKS):
+        w_copy(c, lane).wait_send()
     for mine, copy in sp_copies + t_copies:
         @pl.when(jnp.logical_not(mine))
         def _(copy=copy):
@@ -414,7 +430,7 @@
             pltpu.VMEM(line + (tok, chunk), bf16),
             pltpu.VMEM(line + (tok, chunk), bf16),
             dma((5,)), dma((n,)), dma((n,)),
-            dma, dma((pair,)), dma,
+            dma((CHUNKS,)), dma((CHUNKS,)), dma,
             dma((groups // 2,)), dma((groups,)), dma, dma((groups // 2,)),
             dma((pair, groups // 2)), dma((n,)), dma, dma((n // 2,)),
             dma(line), dma(line), dma(line), dma(line),

time: 62.2 us -> 67.2 us (1.080)
  the two profiles are of different devices: /device:TPU:15 before, /device:TPU:0 now
where the time goes in v6:
time: 67.2 us; the launch traced here: 66.2 us
  Pallas kernels  64.5 us (96%)
  local copies, waits for them, and re-layouts  1.72 us (3%)
    pallas_call x1, Pallas kernels, kernel_body(): pl.pallas_call(functools.partial(layer_kernel, n, groups), out_shape=jax....  64.5 us
    unnamed x1, local copies, waits for them, and re-layouts  1.72 us

profile of v6, /device:TPU:0, one launch (start us, length us, event | category | flops | bytes accessed | tf_op | source)
XLA Modules:
  0.0 66.2 jit_solution(14547500571403336237)
XLA Ops:
  0.0 64.5 %shard_map.64 = bf16[128,1280]{1,0:T(8,128)(2,1)} custom-call(s32[20]{0:T(128)} %class_hbm.1, s32[1,4]{1,0:T(1,128)} %len_hbm.1, bf16[128,640]{1,0:T(8,128)(2,1)} %q_hbm.1, bf16[128,640]{1,0:T(8,128)(2,1)} %k_hbm.1, bf16[128,640]{1,0:T(8,128)(2,1)} %v_hbm.1, bf16[320,1280]{1,0:T(8,128)(2,1)} %w_ref.1), custom_call_target="tpu_custom_call" | custom-call | flops 838860800 | bytes 1638400 | tf_op jit(solution)/shard_map/pallas_call | solution.py:408
  64.5 1.7 %copy.8 = bf16[128,1280]{1,0:T(8,128)(2,1)} copy(bf16[128,1280]{1,0:T(8,128)(2,1)} %shard_map.64) | data formatting | bytes 655360

commit v7 on v5

--- a/solution.py
+++ b/solution.py
@@ -208,12 +208,10 @@
 
     other = plane * pair + (1 - lane)
 
-    def w_copy(c, owner):
-        cols = pl.ds(c * chunk, chunk)
-        return send(w_ref.at[:, cols], w_all.at[owner, :, cols], w_s.at[c], w_r.at[c], other, head)
-
-    for c in range(CHUNKS):
-        w_copy(c, lane).start()
+    def w_copy(owner):
+        return send(w_ref, w_all.at[owner], w_s, w_r, other, head)
+
+    w_copy(lane).start()
 
     loads[4].wait()
     def window_of(axis):
@@ -327,9 +325,9 @@
             mixed[z, :, h * HD:(h + 1) * HD] = value
 
     own_w.wait()
+    w_copy(1 - lane).wait_recv()
 
     def multiply(c):
-        w_copy(c, 1 - lane).wait_recv()
         weight = w_all[:, :, c * chunk:(c + 1) * chunk].reshape(pair * rows, chunk)
         result = jnp.dot(
             mixed[...].reshape(groups * tok, columns), weight, preferred_element_type=jnp.float32
@@ -355,9 +353,10 @@
             sign, came, goes, s_sem, r_sem = way
             send(goes.at[d, c], came.at[d, c], s_sem.at[d, c], r_sem.at[d, c], seq, head).wait_recv()
 
-    for c in range(CHUNKS):
-        multiply(c)
-        for d in range(groups - 1, 0, -1):
+    for d in range(groups - 1, 0, -1):
+        for c in range(CHUNKS):
+            if d == groups - 1:
+                multiply(c)
             for way in ways:
                 @pl.when(reaches(way, d))
                 def _(way=way, d=d, c=c):
@@ -376,8 +375,7 @@
 
     for copy in qkv:
         copy.wait_send()
-    for c in range(CHUNKS):
-        w_copy(c, lane).wait_send()
+    w_copy(lane).wait_send()
     for step in range(1, groups):
         spatial_copy(step).wait_send()
 
@@ -431,7 +429,7 @@
             pltpu.VMEM(line + (tok, chunk), bf16),
             pltpu.VMEM(line + (tok, chunk), bf16),
             dma((5,)), dma((n,)), dma((n,)),
-            dma((CHUNKS,)), dma((CHUNKS,)), dma,
+            dma, dma, dma,
             dma((groups,)), dma((groups,)), dma((3,)), dma((groups,)),
             dma((pair, groups // 2)), dma((n,)), dma((n // 2,)),
             dma(line), dma(line), dma(line), dma(line),

time: 63.6 us -> 58 us (0.912)
  Pallas kernels: 61.7 us -> 55.9 us
    pallas_call x1, Pallas kernels: 61.7 us -> 55.9 us  [kernel_body(): pl.pallas_call(functools.partial(layer_kernel, n, groups), out_shape=jax....]
where the time goes in v7:
time: 58 us; the launch traced here: 57.6 us
  Pallas kernels  55.9 us (96%)
  local copies, waits for them, and re-layouts  1.72 us (3%)
    pallas_call x1, Pallas kernels, kernel_body(): pl.pallas_call(functools.partial(layer_kernel, n, groups), out_shape=jax....  55.9 us
    unnamed x1, local copies, waits for them, and re-layouts  1.72 us

profile of v7, /device:TPU:0, one launch (start us, length us, event | category | flops | bytes accessed | tf_op | source)
XLA Modules:
  0.0 57.6 jit_solution(384679009159948367)
XLA Ops:
  0.0 55.9 %shard_map.64 = bf16[128,1280]{1,0:T(8,128)(2,1)} custom-call(s32[20]{0:T(128)} %class_hbm.1, s32[1,4]{1,0:T(1,128)} %len_hbm.1, bf16[128,640]{1,0:T(8,128)(2,1)} %q_hbm.1, bf16[128,640]{1,0:T(8,128)(2,1)} %k_hbm.1, bf16[128,640]{1,0:T(8,128)(2,1)} %v_hbm.1, bf16[320,1280]{1,0:T(8,128)(2,1)} %w_ref.1), custom_call_target="tpu_custom_call" | custom-call | flops 838860800 | bytes 1638400 | tf_op jit(solution)/shard_map/pallas_call | solution.py:407
  55.9 1.7 %copy.8 = bf16[128,1280]{1,0:T(8,128)(2,1)} copy(bf16[128,1280]{1,0:T(8,128)(2,1)} %shard_map.64) | data formatting | bytes 655360

commit v8 on v7

--- a/solution.py
+++ b/solution.py
@@ -128,7 +128,7 @@
     class_ref, len_ref, q_ref, k_ref, v_ref,
     packed, landed, spat, spat_in, tsend, temp_in, mixed, w_all, partial,
     up_in, up_out, down_in, down_out,
-    load_s, qkv_s, qkv_r, w_s, w_r, w_l, sp_s, sp_r, share_s, share_r, t_s, t_r, tf_s,
+    load_s, qkv_s, qkv_r, w_s, w_r, w_l, sp_s, sp_r, share_s, share_r, t_s, t_r, ts_s, ts_r,
     up_s, up_r, down_s, down_r,
 ):
     pair = n // groups
@@ -267,22 +267,21 @@
         for f in range(n):
             tsend[f % pair, f // pair, :, t * HD:(t + 1) * HD] = result[f * width:(f + 1) * width]
 
-    t_core = lax.rem(seq, 2)
+    t_head, t_slot = lax.rem(seq, groups), seq // groups
     t_copies = []
     for x in range(pair):
-        for y in range(groups // 2):
-            to_seq, to_head = head * pair + x, 2 * y + t_core
-            mine = (to_seq == seq) & (to_head == head)
-            copy = send(tsend.at[x], temp_in.at[seq], t_s.at[x, y], t_r.at[seq], to_seq, to_head)
-            t_copies.append((mine, copy))
-
-            @pl.when(jnp.logical_not(mine))
-            def _(copy=copy):
-                copy.start()
-
-            @pl.when(mine)
-            def _(x=x):
-                temp_in[seq] = tsend[x]
+        to_seq = head * pair + x
+        mine = (to_seq == seq) & (t_head == head)
+        copy = send(tsend.at[x], temp_in.at[t_head, t_slot], t_s.at[x], t_r.at[seq], to_seq, t_head)
+        t_copies.append((mine, copy))
+
+        @pl.when(jnp.logical_not(mine))
+        def _(copy=copy):
+            copy.start()
+
+        @pl.when(mine)
+        def _(x=x):
+            temp_in[t_head, t_slot] = tsend[x]
 
     def share(which, slot, to_head):
         return send(spat_in.at[which], spat_in.at[which], share_s.at[slot], share_r.at[which], seq, to_head)
@@ -295,32 +294,43 @@
     share(head, 0, across).start()
     share(head, 1, sibling).start()
 
-    forwards = [share(head, 0, across), share(head, 1, sibling), share(across, 2, sibling)]
-    for j in range(n // 2):
-        source = 2 * j + core
-        here = (source == seq) & (plane == head)
-        copy = send(temp_in.at[source], temp_in.at[source], tf_s.at[j], t_r.at[source], seq, sibling)
-
-        @pl.when(jnp.logical_not(here))
-        def _(copy=copy):
-            copy.wait_recv()
-
-        copy.start()
-        forwards.append(copy)
+    def t_share(which, slot, to_head):
+        return send(temp_in.at[which], temp_in.at[which], ts_s.at[slot], ts_r.at[which], seq, to_head)
+
+    for j in range(n // groups):
+        source = j * groups + head
+
+        @pl.when(jnp.logical_not(at_home & (source == seq)))
+        def _(j=j, source=source):
+            send(tsend.at[0], temp_in.at[head, j], t_s.at[0], t_r.at[source], seq, head).wait_recv()
+
+    t_share(head, 0, across).start()
+    t_share(head, 1, sibling).start()
+
     share(across, 0, across).wait_recv()
     share(across, 2, sibling).start()
+    t_share(across, 0, across).wait_recv()
+    t_share(across, 2, sibling).start()
+    beyond = lax.rem(sibling + groups // 2, groups)
     share(sibling, 1, sibling).wait_recv()
-    share(lax.rem(sibling + groups // 2, groups), 2, sibling).wait_recv()
-    for j in range(n // 2):
-        source = 2 * j + 1 - core
-        send(temp_in.at[source], temp_in.at[source], tf_s.at[j], t_r.at[source], seq, sibling).wait_recv()
+    share(beyond, 2, sibling).wait_recv()
+    t_share(sibling, 1, sibling).wait_recv()
+    t_share(beyond, 2, sibling).wait_recv()
+    forwards = [share(head, 0, across), share(head, 1, sibling), share(across, 2, sibling)]
+    forwards += [t_share(head, 0, across), t_share(head, 1, sibling), t_share(across, 2, sibling)]
 
     taken = slot_conditions(class_ref, plane * local_heads, local_heads)
     for z in range(groups):
         for h in range(local_heads):
             value = spat_in[:, z, :, h * HD:(h + 1) * HD].reshape(tok, HD)
             for t in range(min(h + 1, TMAX)):
-                slot = temp_in[:, z, :, t * HD:(t + 1) * HD].reshape(tok, HD)
+                slot = jnp.concatenate(
+                    [
+                        temp_in[:, j, z, :, t * HD:(t + 1) * HD].reshape(groups * width, HD)
+                        for j in range(n // groups)
+                    ],
+                    axis=0,
+                )
                 value = jnp.where(taken[h][t], slot, value)
             mixed[z, :, h * HD:(h + 1) * HD] = value
 
@@ -420,7 +430,7 @@
             pltpu.VMEM((groups, quarter, columns), bf16),
             pltpu.VMEM((groups, groups, quarter, columns), bf16),
             pltpu.VMEM((pair, groups, width, TMAX * HD), bf16),
-            pltpu.VMEM((n, groups, width, TMAX * HD), bf16),
+            pltpu.VMEM((groups, n // groups, groups, width, TMAX * HD), bf16),
             pltpu.VMEM((groups, tok, columns), bf16),
             pltpu.VMEM((pair, rows, out_columns), bf16),
             pltpu.VMEM((CHUNKS, groups, tok, chunk), jnp.float32),
@@ -431,7 +441,7 @@
             dma((5,)), dma((n,)), dma((n,)),
             dma, dma, dma,
             dma((groups,)), dma((groups,)), dma((3,)), dma((groups,)),
-            dma((pair, groups // 2)), dma((n,)), dma((n // 2,)),
+            dma((pair,)), dma((n,)), dma((3,)), dma((groups,)),
             dma(line), dma(line), dma(line), dma(line),
         ],
         compiler_params=pltpu.CompilerParams(

time: 58 us -> 58.9 us (1.016)
  the two profiles are of different devices: /device:TPU:0 before, /device:TPU:15 now
where the time goes in v8:
time: 58.9 us; the launch traced here: 58.7 us
  Pallas kernels  57 us (97%)
  local copies, waits for them, and re-layouts  1.72 us (3%)
    pallas_call x1, Pallas kernels, kernel_body(): pl.pallas_call(functools.partial(layer_kernel, n, groups), out_shape=jax....  57 us
    unnamed x1, local copies, waits for them, and re-layouts  1.72 us

profile of v8, /device:TPU:15, one launch (start us, length us, event | category | flops | bytes accessed | tf_op | source)
XLA Modules:
  0.0 58.7 jit_solution(12261879091755290780)
XLA Ops:
  0.0 57.0 %shard_map.64 = bf16[128,1280]{1,0:T(8,128)(2,1)} custom-call(s32[20]{0:T(128)} %class_hbm.1, s32[1,4]{1,0:T(1,128)} %len_hbm.1, bf16[128,640]{1,0:T(8,128)(2,1)} %q_hbm.1, bf16[128,640]{1,0:T(8,128)(2,1)} %k_hbm.1, bf16[128,640]{1,0:T(8,128)(2,1)} %v_hbm.1, bf16[320,1280]{1,0:T(8,128)(2,1)} %w_ref.1), custom_call_target="tpu_custom_call" | custom-call | flops 838860800 | bytes 1638400 | tf_op jit(solution)/shard_map/pallas_call | solution.py:417
  57.0 1.7 %copy.8 = bf16[128,1280]{1,0:T(8,128)(2,1)} copy(bf16[128,1280]{1,0:T(8,128)(2,1)} %shard_map.64) | data formatting | bytes 655360

commit v9 on v7

--- a/solution.py
+++ b/solution.py
@@ -113,12 +113,12 @@
     ]
 
 
-def slot_conditions(class_ref, first, local_heads):
+def slot_conditions(class_ref, first, local_heads, wanted, slots):
     rank = jnp.int32(0)
     taken = []
     for h in range(local_heads):
-        flag = (class_ref[first + h] == 1).astype(jnp.int32)
-        taken.append([flag * (rank == t).astype(jnp.int32) == 1 for t in range(TMAX)])
+        flag = (class_ref[first + h] == wanted).astype(jnp.int32)
+        taken.append([flag * (rank == t).astype(jnp.int32) == 1 for t in range(slots)])
         rank = rank + flag
     return taken
 
@@ -140,6 +140,7 @@
     tok, columns = q_ref.shape
     local_heads = columns // HD
     width, quarter = tok // n, tok // groups
+    spatial_slots = local_heads - 1
     chunk = w_ref.shape[1] // CHUNKS
     rows = w_ref.shape[0]
     scaling = 1.0 / math.sqrt(HD)
@@ -179,7 +180,7 @@
     for load in loads[:4]:
         load.wait()
 
-    taken = slot_conditions(class_ref, head * local_heads, local_heads)
+    taken = slot_conditions(class_ref, head * local_heads, local_heads, 1, TMAX)
     for a, ref in enumerate((q_ref, k_ref, v_ref)):
         for t in range(TMAX):
             value = jnp.zeros((tok, HD), jnp.bfloat16)
@@ -228,8 +229,12 @@
     results = masked_attention(
         [(q_ref[:, at], k_ref[:, at], v_ref[:, at]) for at in spans], same_window, scaling
     )
-    for at, value in zip(spans, results):
-        spat[:, :, at] = value.reshape(groups, quarter, HD)
+    others = slot_conditions(class_ref, head * local_heads, local_heads, 0, spatial_slots)
+    for u in range(spatial_slots):
+        value = jnp.zeros((tok, HD), jnp.bfloat16)
+        for h in range(u, local_heads):
+            value = jnp.where(others[h][u], results[h], value)
+        spat[:, :, spans[u]] = value.reshape(groups, quarter, HD)
 
     at_home = plane == head
 
@@ -315,10 +320,14 @@
         source = 2 * j + 1 - core
         send(temp_in.at[source], temp_in.at[source], tf_s.at[j], t_r.at[source], seq, sibling).wait_recv()
 
-    taken = slot_conditions(class_ref, plane * local_heads, local_heads)
+    taken = slot_conditions(class_ref, plane * local_heads, local_heads, 1, TMAX)
+    others = slot_conditions(class_ref, plane * local_heads, local_heads, 0, spatial_slots)
     for z in range(groups):
         for h in range(local_heads):
-            value = spat_in[:, z, :, h * HD:(h + 1) * HD].reshape(tok, HD)
+            value = jnp.zeros((tok, HD), jnp.bfloat16)
+            for u in range(min(h + 1, spatial_slots)):
+                slot = spat_in[:, z, :, u * HD:(u + 1) * HD].reshape(tok, HD)
+                value = jnp.where(others[h][u], slot, value)
             for t in range(min(h + 1, TMAX)):
                 slot = temp_in[:, z, :, t * HD:(t + 1) * HD].reshape(tok, HD)
                 value = jnp.where(taken[h][t], slot, value)
@@ -371,7 +380,7 @@
         for way in ways:
             arrive(way, 0, c)
             total = total + way[1][0, c].astype(jnp.float32)
-        out_ref[:, c * chunk:(c + 1) * chunk] = total.astype(jnp.bfloat16)
+        out_ref[:, c * chunk:(c + 1) * chunk] = total
 
     for copy in qkv:
         copy.wait_send()
@@ -406,7 +415,7 @@
     line = (groups - 1, CHUNKS)
     return pl.pallas_call(
         functools.partial(layer_kernel, n, groups),
-        out_shape=jax.ShapeDtypeStruct((tok, out_columns), bf16),
+        out_shape=jax.ShapeDtypeStruct((tok, out_columns), jnp.float32),
         in_specs=[pl.BlockSpec(memory_space=pl.ANY)] * 6,
         out_specs=pl.BlockSpec(memory_space=pltpu.VMEM),
         scratch_shapes=[
@@ -417,8 +426,8 @@
             pltpu.VMEM((tok, columns), bf16),
             pltpu.VMEM((n, width, 3 * TMAX * HD), bf16),
             pltpu.VMEM((n, width, 3 * TMAX * HD), bf16),
-            pltpu.VMEM((groups, quarter, columns), bf16),
-            pltpu.VMEM((groups, groups, quarter, columns), bf16),
+            pltpu.VMEM((groups, quarter, columns - HD), bf16),
+            pltpu.VMEM((groups, groups, quarter, columns - HD), bf16),
             pltpu.VMEM((pair, groups, width, TMAX * HD), bf16),
             pltpu.VMEM((n, groups, width, TMAX * HD), bf16),
             pltpu.VMEM((groups, tok, columns), bf16),
@@ -442,7 +451,7 @@
             bytes_accessed=4 * rows * out_columns,
             transcendentals=local_count(columns) * tok * tok,
         ),
-    )(head_class, window_lengths, queries, keys, values, out_weight)
+    )(head_class, window_lengths, queries, keys, values, out_weight).astype(bf16)
 
 
 def local_count(columns):

time: 58 us -> 58.4 us (level)
  other arithmetic: 0 us -> 1.85 us
  local copies, waits for them, and re-layouts: 1.72 us -> 0 us
    convert_element_type x0 -> x1, other arithmetic: none -> 1.85 us  [kernel_body(): return pl.pallas_call(functools.partial(layer_kernel, n, groups), out_sha...]
    unnamed x1 -> x0, local copies, waits for them, and re-layouts: 1.72 us -> none
where the time goes in v9:
time: 58.4 us; the launch traced here: 58.1 us
  Pallas kernels  56.2 us (96%)
  other arithmetic  1.85 us (3%)
    pallas_call x1, Pallas kernels, kernel_body(): pl.pallas_call(functools.partial(layer_kernel, n, groups), out_shape=jax....  56.2 us
    convert_element_type x1, other arithmetic, kernel_body(): return pl.pallas_call(functools.partial(layer_kernel, n, groups), out_sha...  1.85 us

profile of v9, /device:TPU:0, one launch (start us, length us, event | category | flops | bytes accessed | tf_op | source)
XLA Modules:
  0.0 58.1 jit_solution(558276973091305664)
XLA Ops:
  0.0 56.2 %shard_map.64 = f32[128,1280]{1,0:T(8,128)} custom-call(s32[20]{0:T(128)} %class_hbm.1, s32[1,4]{1,0:T(1,128)} %len_hbm.1, bf16[128,640]{1,0:T(8,128)(2,1)} %q_hbm.1, bf16[128,640]{1,0:T(8,128)(2,1)} %k_hbm.1, bf16[128,640]{1,0:T(8,128)(2,1)} %v_hbm.1, bf16[320,1280]{1,0:T(8,128)(2,1)} %w_ref.1), custom_call_target="tpu_custom_call" | custom-call | flops 838860800 | bytes 1638400 | tf_op jit(solution)/shard_map/pallas_call | solution.py:416
  56.3 1.8 %convert_element_type.3 = bf16[128,1280]{1,0:T(8,128)(2,1)} convert(f32[128,1280]{1,0:T(8,128)} %shard_map.64) | non-fusion elementwise | flops 163840 | bytes 983040 | tf_op jit(solution)/shard_map/convert_element_type | solution.py:454
